TPU v7x, 512 devices: a whole 4x4x16 slice. The times are simulated.
512 devices in a mesh: group: 8 (over x, core), shard: 16 (over z_hi, y), col: 4 (over z_lo).
Axes of the slice: x: 4, y: 4, z: 16 (z_hi: 4, z_lo: 4; z = z_hi * 4 + z_lo), core: 2. Of those that a mesh axis runs over, the one named last changes fastest.
Arguments:
- master: bfloat16 [4, 1024, 5120], P('col', 'group', 'shard'), may hold values from -0.09375 to 0.09375
- grad: bfloat16 [4, 1024, 5120], P('col', 'group', 'shard'), may hold values from -6 to 6
- first: bfloat16 [4, 1024, 5120], P('col', 'group', 'shard'), may hold values from -0.59765625 to 0.59765625
- second: bfloat16 [4, 1024, 5120], P('col', 'group', 'shard'), may hold values from 0.0009994507 to 1
- resident: bfloat16 [8, 4096, 5120], P('group', 'col', 'shard'), may hold values from -0.09375 to 0.09375
- tags: int32 [8], P('group'), may hold values from 0 to 15, as said below
- queries: bfloat16 [8, 4, 4096], P('group', None, 'col'), may hold values from -70 to 70
- key_cache: bfloat16 [8, 4, 8192, 1024], P('group', None, 'shard', 'col'), may hold values from -8 to 8
- value_cache: bfloat16 [8, 4, 8192, 1024], P('group', None, 'shard', 'col'), may hold values from -6 to 6
- lengths: int32 [8, 4], P('group'), may hold values from 1024 to 8192, as said below
Outputs:
- new_master: bfloat16 [4, 1024, 5120], P('col', 'group', 'shard')
- new_first: bfloat16 [4, 1024, 5120], P('col', 'group', 'shard')
- new_second: bfloat16 [4, 1024, 5120], P('col', 'group', 'shard')
- projected: bfloat16 [8, 4, 5120], P('group', None, 'shard')
Inputs may be any that keep to these rules, and one draw needn't show every extreme that they name: `tags`: at least one replica has an odd version and at least one an even version; some replica has version 15. `lengths`: some row has exactly 8192.
All inputs are finite; a program needn't handle non-finite values.
Results may differ from a plain program's by a relative error of at most 0.012.
Values may be sent and summed in bfloat16 or wider, within the bound.
A program may use at most 64 MiB of HBM per device.

v0:
```python
import jax
import jax.numpy as jnp
from jax import lax
from jax.sharding import PartitionSpec as P

HS = 128


beta_one = 0.9
beta_two = 0.999
learn_rate = 0.01
decay = 0.1
adam_eps = 1e-08
correct_one = 1.0
correct_two = 0.6323045752
neg_big = -1e30


def merged(value, axis, join):
    pieces = jax.tree.map(lambda part: lax.all_gather(part, axis), value)
    head = jax.tree.map(lambda part: part[0], pieces)
    tail = jax.tree.map(lambda part: part[1:], pieces)
    so_far, _ = lax.scan(lambda so_far, share: (join(so_far, share), None), head, tail)
    return so_far


def combine(left, right):
    best = jnp.maximum(left[0], right[0])
    left_factor = jnp.exp(left[0] - best)
    right_factor = jnp.exp(right[0] - best)
    total = left[1] * left_factor + right[1] * right_factor
    accum = left[2] * left_factor[..., None] + right[2] * right_factor[..., None]
    return (best, total, accum)


def per_device(
    master, grad, first, second, resident, tags, queries, key_cache, value_cache, lengths
):
    g32 = grad.astype(jnp.float32)
    first_new = beta_one * first.astype(jnp.float32) + (1.0 - beta_one) * g32
    second_new = beta_two * second.astype(jnp.float32) + (1.0 - beta_two) * g32 * g32
    w32 = master.astype(jnp.float32)
    step_size = (
        learn_rate * (first_new / correct_one) / (jnp.sqrt(second_new / correct_two) + adam_eps)
    )
    updated = (w32 - step_size - learn_rate * decay * w32).astype(jnp.bfloat16)
    rows = queries.shape[1]
    width = queries.shape[2]
    span = key_cache.shape[2]
    kv_local = key_cache.shape[3] // HS
    per_kv = width // kv_local // HS
    query = queries[0].reshape(rows, kv_local, per_kv, HS)
    keys = key_cache[0].reshape(rows, span, kv_local, HS)
    values = value_cache[0].reshape(rows, span, kv_local, HS)
    position = lax.axis_index("shard") * span + jnp.arange(span, dtype=jnp.int32)
    valid = position[None, :] < lengths[0][:, None]
    mask = valid[:, None, None, :]
    scores = jnp.einsum("rkgd,rpkd->rkgp", query, keys, preferred_element_type=jnp.float32) * (
        1.0 / HS**0.5
    )
    local_best = jnp.max(jnp.where(mask, scores, neg_big), axis=-1)
    probs = jnp.where(mask, jnp.exp(scores - local_best[..., None]), 0.0)
    local_total = jnp.sum(probs, axis=-1)
    local_accum = jnp.einsum(
        "rkgp,rpkd->rkgd", probs.astype(jnp.bfloat16), values, preferred_element_type=jnp.float32
    )
    best, total, accum = merged((local_best, local_total, local_accum), "shard", combine)
    attended = (accum / total[..., None]).astype(jnp.bfloat16).reshape(rows, width)
    fresh = jnp.dot(
        attended,
        lax.all_gather(updated, "group", axis=1, tiled=True)[0],
        preferred_element_type=jnp.float32,
    )
    stale = jnp.dot(attended, resident[0], preferred_element_type=jnp.float32)
    share = jnp.where(tags[0] % 2 == 1, fresh, stale)
    projected = lax.psum(share, "col").astype(jnp.bfloat16)[None]
    return (updated, first_new.astype(jnp.bfloat16), second_new.astype(jnp.bfloat16), projected)


def solution(mesh):
    return jax.shard_map(
        per_device,
        mesh=mesh,
        in_specs=(
            P("col", "group", "shard"),
            P("col", "group", "shard"),
            P("col", "group", "shard"),
            P("col", "group", "shard"),
            P("group", "col", "shard"),
            P("group"),
            P("group", None, "col"),
            P("group", None, "shard", "col"),
            P("group", None, "shard", "col"),
            P("group", None),
        ),
        out_specs=(
            P("col", "group", "shard"),
            P("col", "group", "shard"),
            P("col", "group", "shard"),
            P("group", None, "shard"),
        ),
        check_vma=False,
    )
```

profile of v0, /device:TPU:6, one launch (start us, length us, event | category | flops | bytes accessed | tf_op | source)
XLA Modules:
  0.0 188.2 jit_solution(18340770299058455969)
XLA Ops:
  0.6 0.0 copy-start
  0.7 0.0 copy-start.10
  0.7 0.7 copy-done.10
  1.4 0.1 broadcast_compare_fusion
  1.5 1.4 reshape_squeeze.10
  2.8 0.0 copy-done.9
  2.8 0.0 copy-start.1
  2.9 0.5 select_reduce_fusion
  3.3 0.7 copy-done.1
  4.1 0.3 reshape_squeeze.11
  4.3 0.3 fusion.3
  4.6 60.3 %all-gather.2 = f32[64,2,4,128]{3,2,1,0:T(4,128)S(1)} all-gather(f32[4,2,4,128]{3,2,1,0:T(4,128)S(1)} %fusion.3), channel_id=4, replica_groups=mesh['group'=8,'shard'=16,'col'=4] {'shard'}, dimensions={0}, use_global_device_ids=true | all-gather | bytes 278528 | tf_op jit(solution)/shard_map/all_gather | solution.py:20
  64.9 0.7 copy-done.2
  65.6 0.2 fusion.16
  65.8 45.5 %all-gather.1 = f32[64,2,4]{2,1,0:T(2,128)S(1)} all-gather(f32[4,2,4]{2,1,0:T(2,128)S(1)} %fusion.16), channel_id=3, replica_groups=mesh['group'=8,'shard'=16,'col'=4] {'shard'}, dimensions={0}, use_global_device_ids=true | all-gather | bytes 2176 | tf_op jit(solution)/shard_map/all_gather | solution.py:20
  111.3 0.6 copy-done.4
  111.9 47.5 %all-gather = f32[64,2,4]{2,1,0:T(2,128)S(1)} all-gather(f32[4,2,4]{2,1,0:T(2,128)S(1)} %get-tuple-element.65), channel_id=2, replica_groups=mesh['group'=8,'shard'=16,'col'=4] {'shard'}, dimensions={0}, use_global_device_ids=true | all-gather | bytes 2176 | tf_op jit(solution)/shard_map/all_gather | solution.py:20
  159.4 0.0 slice-start.1
  159.4 0.7 slice-done
  160.1 0.2 slice-done.1
  160.3 2.2 %while.14 = (s32[]{:T(128)}, f32[4,2,4]{2,1,0:T(2,128)S(1)}, f32[4,2,4]{2,1,0:T(2,128)S(1)}, f32[4,2,4,128]{3,2,1,0:T(4,128)S(1)}, f32[15,4,2,4]{3,2,1,0:T(2,128...) while((s32[]{:T(128)}, f32[4,2,4]{2,1,0:T(2,128)S(1)}, ...), condition=%wide.region_3.4_spmd, body=%wide.region_2.3_spmd.sunk | while | flops 12482 | bytes 50525 | solution.py:23
  160.4 0.1 fusion.29
  160.5 0.1 fusion.29
  160.7 0.1 fusion.29
  160.8 0.1 fusion.29
  160.9 0.1 fusion.29
  161.1 0.1 fusion.29
  161.2 0.1 fusion.29
  161.4 0.1 fusion.29
  161.5 0.1 fusion.29
  161.7 0.1 fusion.29
  161.8 0.1 fusion.29
  162.0 0.1 fusion.29
  162.1 0.1 fusion.29
  162.3 0.1 fusion.29
  162.4 0.1 fusion.29
  162.5 0.1 divide_convert_fusion
  162.6 0.0 copy-done.8
  162.6 0.0 copy-done.7
  162.7 0.0 copy-done.5
  162.7 0.0 copy-done.6
  162.7 0.8 fusion.14
  163.5 12.5 %all_gather.27 = bf16[1,1024,320]{1,2,0:T(8,128)(2,1)S(1)} all-gather(bf16[1,128,320]{1,2,0:T(8,128)(2,1)S(1)} %get-tuple-element.63), channel_id=1, replica_groups=mesh['group'=8,'shard'=16,'col'=4] {'group'}, dimensions={1}, use_global_device_ids=true | all-gather | bytes 737280 | tf_op jit(solution)/shard_map/all_gather | solution.py:71
  176.0 0.0 copy-done.3
  176.0 0.3 fusion.7
  177.0 0.0 copy-done
  177.0 0.3 convolution_select_fusion
  177.3 10.9 %psum.7 = bf16[4,320]{1,0:T(4,128)(2,1)} all-reduce(f32[4,320]{1,0:T(4,128)S(1)} %convolution_select_fusion), channel_id=1, replica_groups=mesh['group'=8,'shard'=16,'col'=4] {'col'}, use_global_device_ids=true, to_apply=%region_4.5 | all-reduce | flops 1280 | bytes 7680 | tf_op jit(solution)/shard_map/psum | solution.py:76
  (31 shorter events, 0.6 us)
Async XLA Ops:
  0.6 176.4 %copy-start = (bf16[1,1024,320]{1,2,0:T(8,128)(2,1)S(1)}, bf16[1,1024,320]{1,2,0:T(8,128)(2,1)}, u32[]{:S(2)}) copy-start(bf16[1,1024,320]{1,2,0:T(8,128)(2,1)} %param.16) | copy-start | bytes 1966084
  0.7 0.7 copy-start.10
  1.5 1.4 copy-start.9
  2.8 1.2 copy-start.1
  64.9 0.7 copy-start.2
  111.3 0.6 copy-start.4
  111.3 51.4 %copy-start.8 = (bf16[1,128,320]{1,2,0:T(8,128)(2,1)S(1)}, bf16[1,128,320]{1,2,0:T(8,128)(2,1)}, u32[]{:S(2)}) copy-start(bf16[1,128,320]{1,2,0:T(8,128)(2,1)} %param.12) | copy-start | bytes 245764
  159.4 0.7 slice-start
  159.4 3.2 %copy-start.7 = (bf16[1,128,320]{1,2,0:T(8,128)(2,1)S(1)}, bf16[1,128,320]{1,2,0:T(8,128)(2,1)}, u32[]{:S(2)}) copy-start(bf16[1,128,320]{1,2,0:T(8,128)(2,1)} %param.14) | copy-start | bytes 245764
  159.4 0.9 slice-start.1
  160.3 2.3 %copy-start.5 = (bf16[1,128,320]{1,2,0:T(8,128)(2,1)S(1)}, bf16[1,128,320]{1,2,0:T(8,128)(2,1)}, u32[]{:S(2)}) copy-start(bf16[1,128,320]{1,2,0:T(8,128)(2,1)} %param.13) | copy-start | bytes 245764
  160.3 2.3 %copy-start.6 = (bf16[1,128,320]{1,2,0:T(8,128)(2,1)S(1)}, bf16[1,128,320]{1,2,0:T(8,128)(2,1)}, u32[]{:S(2)}) copy-start(bf16[1,128,320]{1,2,0:T(8,128)(2,1)} %param.15) | copy-start | bytes 245764
  163.5 12.5 %copy-start.3 = (bf16[1,128,320]{1,2,0:T(8,128)(2,1)}, bf16[1,128,320]{1,2,0:T(8,128)(2,1)S(1)}, u32[]{:S(2)}) copy-start(bf16[1,128,320]{1,2,0:T(8,128)(2,1)S(1)} %get-tuple-element.63) | copy-start | bytes 245764
where the time goes:
time: 189 us; the launch traced here: 188 us
  blocking collectives  177 us (94%)
  local copies, waits for them, and re-layouts  5.35 us (3%)
  other arithmetic  3.19 us (2%)
    all_gather x3, blocking collectives, merged(): pieces = jax.tree.map(lambda part: lax.all_gather(part, axis), value)  153 us
    all_gather x1, blocking collectives, per_device(): lax.all_gather(updated, 'group', axis=1, tiled=True)[0]  12.5 us
    psum x1, blocking collectives, per_device(): projected = lax.psum(share, 'col').astype(jnp.bfloat16)[None]  10.9 us

commit v1 on v0

v1 whole, which is shorter than its diff:
```python
import functools

import jax
import jax.numpy as jnp
from jax import lax
from jax.experimental import pallas as pl
from jax.experimental.pallas import tpu as pltpu
from jax.sharding import PartitionSpec as P

HS = 128
MESH = pl.DeviceIdType.MESH
F32 = jnp.float32
BF16 = jnp.bfloat16

beta_one = 0.9
beta_two = 0.999
learn_rate = 0.01
decay = 0.1
adam_eps = 1e-08
correct_one = 1.0
correct_two = 0.6323045752
neg_big = -1e30


def adam(master, grad, first, second):
    g32 = grad.astype(F32)
    first_new = beta_one * first.astype(F32) + (1.0 - beta_one) * g32
    second_new = beta_two * second.astype(F32) + (1.0 - beta_two) * g32 * g32
    w32 = master.astype(F32)
    step_size = (
        learn_rate * (first_new / correct_one) / (jnp.sqrt(second_new / correct_two) + adam_eps)
    )
    updated = w32 - step_size - learn_rate * decay * w32
    return updated.astype(BF16), first_new.astype(BF16), second_new.astype(BF16)


def nt(a, b):
    return lax.dot_general(a, b, (((1,), (1,)), ((), ())), preferred_element_type=F32)


def pack(acc, best, total):
    lane = lax.broadcasted_iota(jnp.int32, acc.shape, 1)
    high = total.astype(BF16).astype(F32)
    stats = jnp.where(lane == 0, best, jnp.where(lane == 1, high, jnp.where(lane == 2, total - high, 0.0)))
    return acc, stats


def merge(shares):
    parts = [shares[i].astype(F32) for i in range(4)]
    bests = [part[8:, 0:1] for part in parts]
    best = jnp.maximum(jnp.maximum(bests[0], bests[1]), jnp.maximum(bests[2], bests[3]))
    acc, total = 0.0, 0.0
    for part, own in zip(parts, bests):
        factor = jnp.exp(own - best)
        acc = acc + part[:8] * factor
        total = total + (part[8:, 1:2] + part[8:, 2:3]) * factor
    return acc, best, total


def kernel(
    master_ref, grad_ref, first_ref, second_ref, resident_ref, tags_ref, queries_ref, keys_ref, values_ref, lengths_ref,
    out_ref,
    master, grad, first, second, resident, tags, queries, keys, values, lengths,
    slabs, chosen, y_out, y_in, z_out, z_in, a_in, c_in,
    load_sem, key_sem, value_sem,
    wx_send, wx_recv, ws_send, ws_recv,
    y_send, y_recv, z_send, z_recv, a_send, a_recv, c_send, c_recv,
):
    group = lax.axis_index("group")
    shard = lax.axis_index("shard")
    col = lax.axis_index("col")
    x, core = group // 2, group % 2
    z, y = shard // 4, shard % 4

    def x_peer(d):
        return {"group": (x + d) % 4 * 2 + core}

    def y_peer(d):
        return {"shard": z * 4 + (y + d) % 4}

    def z_peer(d):
        return {"shard": (z + d) % 4 * 4 + y}

    def c_peer(d):
        return {"col": (col + d) % 4}

    sibling = {"group": x * 2 + 1 - core}

    def load(i, src, dst):
        copy = pltpu.make_async_copy(src, dst, load_sem.at[i])
        copy.start()
        return copy

    q_load = load(0, queries_ref, queries)
    l_load = load(1, lengths_ref, lengths)
    k_loads = [pltpu.make_async_copy(keys_ref.at[0, r], keys.at[r], key_sem.at[r]) for r in range(4)]
    v_loads = [pltpu.make_async_copy(values_ref.at[0, r], values.at[r], value_sem.at[r]) for r in range(4)]
    w_loads = [
        load(2 + i, src, dst)
        for i, (src, dst) in enumerate(
            ((master_ref, master), (grad_ref, grad), (first_ref, first), (second_ref, second))
        )
    ]
    for copy in k_loads + v_loads:
        copy.start()
    r_load = load(6, resident_ref, resident)
    t_load = load(7, tags_ref, tags)

    barrier = pltpu.get_barrier_semaphore()
    for d in (1, 2, 3):
        for peer in (x_peer(d), y_peer(d), z_peer(d), c_peer(d)):
            pl.semaphore_signal(barrier, inc=1, device_id=peer, device_id_type=MESH)
    pl.semaphore_signal(barrier, inc=1, device_id=sibling, device_id_type=MESH)

    for copy in w_loads:
        copy.wait()
    slabs[group] = adam(master[0], grad[0], first[0], second[0])[0]
    pl.semaphore_wait(barrier, 13)

    def send(src, dst, send_sem, recv_sem, peer):
        copy = pltpu.make_async_remote_copy(
            src_ref=src, dst_ref=dst, send_sem=send_sem, recv_sem=recv_sem, device_id=peer, device_id_type=MESH
        )
        copy.start()
        return copy

    own_w = [send(slabs.at[group], slabs.at[group], ws_send.at[0], ws_recv.at[0], sibling)]
    for d in (1, 3, 2):
        own_w.append(send(slabs.at[group], slabs.at[group], wx_send.at[d - 1], wx_recv.at[d - 1], x_peer(d)))

    q_load.wait()
    l_load.wait()
    q32 = queries[0].astype(F32)
    tall = [jnp.concatenate([q32[:, h * HS : (h + 1) * HS] for h in range(4 * k, 4 * k + 4)], axis=0) for k in (0, 1)]
    blank = jnp.zeros((16, HS), F32)
    wide = jnp.concatenate(
        [jnp.concatenate([tall[0], blank], axis=1), jnp.concatenate([blank, tall[1]], axis=1)], axis=0
    )
    row_q = lax.broadcasted_iota(jnp.int32, (32, 2 * HS), 0) % 4
    scores = jnp.zeros((32, 512), F32)
    for r in range(4):
        k_loads[r].wait()
        scores = scores + nt(jnp.where(row_q == r, wide, 0.0).astype(BF16), keys[r])
    scores = scores * (1.0 / HS**0.5)
    row = lax.broadcasted_iota(jnp.int32, (32, 512), 0) % 4
    position = shard * 512 + lax.broadcasted_iota(jnp.int32, (32, 512), 1)
    limit = jnp.where(
        row == 0, lengths[0, 0], jnp.where(row == 1, lengths[0, 1], jnp.where(row == 2, lengths[0, 2], lengths[0, 3]))
    )
    mask = position < limit
    best = jnp.max(jnp.where(mask, scores, neg_big), axis=1, keepdims=True)
    best = best.astype(BF16).astype(F32)
    probs = jnp.where(mask, jnp.exp(scores - best), 0.0)
    total = jnp.sum(probs, axis=1, keepdims=True)
    both = jnp.zeros((32, 2 * HS), F32)
    for r in range(4):
        v_loads[r].wait()
        both = both + jnp.dot(
            jnp.where(row == r, probs, 0.0).astype(BF16), values[r], preferred_element_type=F32
        )
    acc = jnp.concatenate([both[:16, :HS], both[16:, HS:]], axis=0)

    acc, stats = pack(acc, best, total)
    for j in range(4):
        y_out[j] = jnp.concatenate([acc[8 * j : 8 * j + 8], stats[8 * j : 8 * j + 8]], axis=0).astype(BF16)
    sent = []
    for d in (2, 1, 3):
        sent.append(send(y_out.at[(y + d) % 4], y_in.at[y], y_send.at[d - 1], y_recv.at[d - 1], y_peer(d)))
    y_in[y] = y_out[y]
    for copy in sent:
        copy.wait_recv()
    acc, best, total = merge(y_in)
    acc, stats = pack(acc, best, total)
    z_out[...] = jnp.concatenate([acc, stats], axis=0).astype(BF16)
    for d in (2, 1, 3):
        sent.append(send(z_out, z_in.at[z], z_send.at[d - 1], z_recv.at[d - 1], z_peer(d)))
    z_in[z] = z_out[...]

    passed = []
    for d in (1, 3, 2):
        own_w[(1, 3, 2).index(d) + 1].wait_recv()
        block = (x + 4 - d) % 4 * 2 + core
        passed.append(send(slabs.at[block], slabs.at[block], ws_send.at[d], ws_recv.at[d], sibling))
    r_load.wait()
    t_load.wait()
    odd = jnp.full((320, HS), tags[0], jnp.int32) % 2 == 1
    own_w[0].wait_recv()
    for copy in passed:
        copy.wait_recv()
    for h in range(8):
        place = (h % 2 * 4 + h // 2) * HS
        chosen[:, place : place + HS] = jnp.where(odd, slabs[h], resident[0, :, h * HS : (h + 1) * HS])

    for copy in sent[3:]:
        copy.wait_recv()
    acc, _, total = merge(z_in)
    a_in[y] = acc / total
    for d in (2, 1, 3):
        sent.append(send(a_in.at[y], a_in.at[y], a_send.at[d - 1], a_recv.at[d - 1], y_peer(d)))
    for copy in sent[6:]:
        copy.wait_recv()
    attended = jnp.concatenate([a_in[j] for j in range(4)], axis=1).astype(BF16)
    even = nt(attended, chosen[:, : 4 * HS])
    uneven = nt(attended, chosen[:, 4 * HS :])
    share = even[:4] + uneven[4:]
    c_in[col] = jnp.concatenate(
        [
            share[:, :HS],
            share[:, HS : 2 * HS],
            jnp.concatenate([share[:, 2 * HS :], jnp.zeros((4, 64), F32)], axis=1),
            jnp.zeros((4, HS), F32),
        ],
        axis=0,
    ).astype(BF16)
    for d in (3, 2, 1):
        sent.append(send(c_in.at[col], c_in.at[col], c_send.at[d - 1], c_recv.at[d - 1], c_peer(d)))
    for copy in sent[9:]:
        copy.wait_recv()
    final = c_in[0].astype(F32) + c_in[1].astype(F32) + c_in[2].astype(F32) + c_in[3].astype(F32)
    out_ref[0] = jnp.concatenate([final[0:4], final[4:8], final[8:12, :64]], axis=1).astype(BF16)
    for copy in own_w + passed + sent:
        copy.wait_send()


def per_device(master, grad, first, second, resident, tags, queries, keys, values, lengths):
    flip = functools.partial(jnp.swapaxes, axis1=1, axis2=2)
    updated, first_new, second_new = adam(master, grad, first, second)
    dma = pltpu.SemaphoreType.DMA
    block = pltpu.VMEM((1, 320, 128), BF16)
    projected = pl.pallas_call(
        kernel,
        out_shape=jax.ShapeDtypeStruct((1, 4, 320), BF16),
        in_specs=[pl.BlockSpec(memory_space=pl.ANY)] * 10,
        out_specs=pl.BlockSpec(memory_space=pltpu.VMEM),
        scratch_shapes=[
            block, block, block, block,
            pltpu.VMEM((1, 320, 1024), BF16),
            pltpu.SMEM((1,), jnp.int32),
            pltpu.VMEM((1, 4, 1024), BF16),
            pltpu.VMEM((4, 512, 256), BF16),
            pltpu.VMEM((4, 512, 256), BF16),
            pltpu.SMEM((1, 4), jnp.int32),
            pltpu.VMEM((8, 320, 128), BF16),
            pltpu.VMEM((320, 1024), BF16),
            pltpu.VMEM((4, 16, 128), BF16),
            pltpu.VMEM((4, 16, 128), BF16),
            pltpu.VMEM((16, 128), BF16),
            pltpu.VMEM((4, 16, 128), BF16),
            pltpu.VMEM((4, 8, 128), F32),
            pltpu.VMEM((4, 16, 128), BF16),
            dma((8,)), dma((4,)), dma((4,)),
            dma((3,)), dma((3,)), dma((4,)), dma((4,)),
            dma((3,)), dma((3,)), dma((3,)), dma((3,)), dma((3,)), dma((3,)), dma((3,)), dma((3,)),
        ],
        compiler_params=pltpu.CompilerParams(collective_id=0, has_side_effects=True),
    )(flip(master), flip(grad), flip(first), flip(second), flip(resident), tags, queries, keys, values, lengths)
    return updated, first_new, second_new, projected


def solution(mesh):
    return jax.shard_map(
        per_device,
        mesh=mesh,
        in_specs=(
            P("col", "group", "shard"),
            P("col", "group", "shard"),
            P("col", "group", "shard"),
            P("col", "group", "shard"),
            P("group", "col", "shard"),
            P("group"),
            P("group", None, "col"),
            P("group", None, "shard", "col"),
            P("group", None, "shard", "col"),
            P("group", None),
        ),
        out_specs=(
            P("col", "group", "shard"),
            P("col", "group", "shard"),
            P("col", "group", "shard"),
            P("group", None, "shard"),
        ),
        check_vma=False,
    )
```

time: 189 us -> 36.7 us (0.19)
  blocking collectives: 177 us -> 0 us
  Pallas kernels: 0 us -> 33 us
  local copies, waits for them, and re-layouts: 5.35 us -> 1.28 us
  other arithmetic: 3.19 us -> 0.87 us
    all_gather x4 -> x0, blocking collectives: 166 us -> none  [the longest x3 153 us: merged(): pieces = jax.tree.map(lambda part: lax.all_gather(part, axis), value)]
    pallas_call x0 -> x1, Pallas kernels: none -> 33 us  [per_device(): pl.pallas_call(kernel, out_shape=jax.ShapeDtypeStruct((1, 4, 320), BF16),...]
    psum x1 -> x0, blocking collectives: 10.9 us -> none  [per_device(): projected = lax.psum(share, 'col').astype(jnp.bfloat16)[None]]
    add x31 -> x0, other arithmetic: 2.04 us -> none  [the longest x15 1.56 us: combine(): left[2] * left_factor[..., None] + right[2] * right_factor[..., None]]
where the time goes in v1:
time: 36.7 us; the launch traced here: 36.5 us
  Pallas kernels  33 us (90%)
  between operations  1.35 us (4%)
  local copies, waits for them, and re-layouts  1.28 us (3%)
  other arithmetic  0.87 us (2%)
    pallas_call x1, Pallas kernels, per_device(): pl.pallas_call(kernel, out_shape=jax.ShapeDtypeStruct((1, 4, 320), BF16),...  33 us
    unnamed x11, local copies, waits for them, and re-layouts  1.28 us
    convert_element_type x1, other arithmetic, adam(): second_new.astype(BF16)  0.87 us

profile of v1, /device:TPU:6, one launch (start us, length us, event | category | flops | bytes accessed | tf_op | source)
XLA Modules:
  0.0 36.5 jit_solution(14659527485665604517)
XLA Ops:
  1.3 0.0 copy-start
  1.3 0.0 copy-start.1
  1.3 0.0 copy-start.2
  1.3 0.0 copy-start.3
  1.3 33.0 %shard_map.129 = bf16[1,4,320]{2,1,0:T(4,128)(2,1)} custom-call(bf16[1,320,128]{2,1,0:T(8,128)(2,1)} %bitcast.9, bf16[1,320,128]{2,1,0:T(8,128)(2,1)} %bitcast.6, bf16[1,320,128]{2,1,0:T(8,128)(2,1)} %bitcast.8, bf16[1,320,128]{2,1,0:T(8,128)(2,1)} %bitcast.7, bf16[1,320,1024]{2,1,0:T(8,128)(2,1)} %bitcast.5, s32[1]{0:T(128)S(6)} %copy.15.tags_ref, ...), custom_call_target="tpu_custom_call" | custom-call | tf_op jit(solution)/shard_map/pallas_call | solution.py:230
  34.3 0.0 copy-done
  34.3 0.0 copy-done.1
  34.4 0.0 copy-done.2
  34.4 0.0 copy-done.3
  34.4 0.9 %fusion.5 = (bf16[1,128,320]{1,2,0:T(8,128)(2,1)}, bf16[1,128,320]{1,2,0:T(8,128)(2,1)}, bf16[1,128,320]{1,2,0:T(8,128)(2,1)}) fusion(bf16[1,128,320]{1,2,0:T(8,128)(2,1)S(1)} %copy-done, bf16[1,128,320]{1,2,0:T(8,128)(2,1)S(1)} %copy-done.1, bf16[1,128,320]{1,2,0:T(8,128)(2,1)S(1)} %copy-done.2, bf16[1,128,320]{1,2,0:T(8,128)(2,1)S(1)} %copy-done.3), kind=kLoop, calls=%fused_computation.9 | loop fusion | flops 860160 | bytes 573440 | tf_op jit(solution)/shard_map/convert_element_type | solution.py:34
  35.2 0.0 copy-start.4
  35.2 0.7 %copy-done.4 = bf16[1,4,320]{2,1,0:T(4,128)(2,1)S(1)} copy-done((bf16[1,4,320]{2,1,0:T(4,128)(2,1)S(1)}, bf16[1,4,320]{2,1,0:T(4,128)(2,1)}, u32[]{:S(2)}) %copy-start.4) | copy-done | bytes 2584
  35.9 0.6 %copy.16 = bf16[1,4,320]{2,1,0:T(4,128)(2,1)} copy(bf16[1,4,320]{2,1,0:T(4,128)(2,1)S(1)} %copy-done.4) | data formatting | bytes 5120
Async XLA Ops:
  1.3 33.1 %copy-start = (bf16[1,128,320]{1,2,0:T(8,128)(2,1)S(1)}, bf16[1,128,320]{1,2,0:T(8,128)(2,1)}, u32[]{:S(2)}) copy-start(bf16[1,128,320]{1,2,0:T(8,128)(2,1)} %param.11) | copy-start | bytes 245764
  1.3 33.1 %copy-start.1 = (bf16[1,128,320]{1,2,0:T(8,128)(2,1)S(1)}, bf16[1,128,320]{1,2,0:T(8,128)(2,1)}, u32[]{:S(2)}) copy-start(bf16[1,128,320]{1,2,0:T(8,128)(2,1)} %param.13) | copy-start | bytes 245764
  1.3 33.1 %copy-start.2 = (bf16[1,128,320]{1,2,0:T(8,128)(2,1)S(1)}, bf16[1,128,320]{1,2,0:T(8,128)(2,1)}, u32[]{:S(2)}) copy-start(bf16[1,128,320]{1,2,0:T(8,128)(2,1)} %param.12) | copy-start | bytes 245764
  1.3 33.1 %copy-start.3 = (bf16[1,128,320]{1,2,0:T(8,128)(2,1)S(1)}, bf16[1,128,320]{1,2,0:T(8,128)(2,1)}, u32[]{:S(2)}) copy-start(bf16[1,128,320]{1,2,0:T(8,128)(2,1)} %param.10) | copy-start | bytes 245764
  35.2 0.7 %copy-start.4 = (bf16[1,4,320]{2,1,0:T(4,128)(2,1)S(1)}, bf16[1,4,320]{2,1,0:T(4,128)(2,1)}, u32[]{:S(2)}) copy-start(bf16[1,4,320]{2,1,0:T(4,128)(2,1)} %shard_map.129) | copy-start | bytes 7684

commit v2 on v1

v2 whole, which is shorter than its diff:
```python
import functools

import jax
import jax.numpy as jnp
from jax import lax
from jax.experimental import pallas as pl
from jax.experimental.pallas import tpu as pltpu
from jax.sharding import PartitionSpec as P

HS = 128
MESH = pl.DeviceIdType.MESH
F32 = jnp.float32
BF16 = jnp.bfloat16

beta_one = 0.9
beta_two = 0.999
learn_rate = 0.01
decay = 0.1
adam_eps = 1e-08
correct_one = 1.0
correct_two = 0.6323045752
neg_big = -1e30


def adam(master, grad, first, second):
    g32 = grad.astype(F32)
    first_new = beta_one * first.astype(F32) + (1.0 - beta_one) * g32
    second_new = beta_two * second.astype(F32) + (1.0 - beta_two) * g32 * g32
    w32 = master.astype(F32)
    step_size = (
        learn_rate * (first_new / correct_one) / (jnp.sqrt(second_new / correct_two) + adam_eps)
    )
    updated = w32 - step_size - learn_rate * decay * w32
    return updated.astype(BF16), first_new.astype(BF16), second_new.astype(BF16)


def nt(a, b):
    return lax.dot_general(a, b, (((1,), (1,)), ((), ())), preferred_element_type=F32)


def pack(acc, best, total):
    lane = lax.broadcasted_iota(jnp.int32, (16, HS), 1)
    high = total.astype(BF16).astype(F32)
    low = total - high
    stats = jnp.zeros((16, HS), F32)
    for i, column in enumerate((best[:16], high[:16], low[:16], best[16:], high[16:], low[16:])):
        stats = jnp.where(lane == i, column, stats)
    return jnp.concatenate([acc, stats], axis=0).astype(BF16)


def merge(shares):
    parts = [shares[i].astype(F32) for i in range(4)]
    bests = [jnp.concatenate([part[32:, 0:1], part[32:, 3:4]], axis=0) for part in parts]
    best = jnp.maximum(jnp.maximum(bests[0], bests[1]), jnp.maximum(bests[2], bests[3]))
    acc, total = 0.0, 0.0
    for part, own in zip(parts, bests):
        factor = jnp.exp(own - best)
        acc = acc + part[:32] * factor
        sums = jnp.concatenate([part[32:, 1:2] + part[32:, 2:3], part[32:, 4:5] + part[32:, 5:6]], axis=0)
        total = total + sums * factor
    return acc, best, total


def kernel(
    master_ref, grad_ref, first_ref, second_ref, resident_ref, tags_ref, queries_ref, keys_ref, values_ref, lengths_ref,
    updated_ref, first_out, second_out, out_ref,
    state, resident, tags, queries, keys, values, lengths,
    slabs, chosen, y_out, y_in, z_out, z_in, c_in,
    z_ready, s_ready, small_sem, key_sem, value_sem, state_sem, resident_sem, tags_sem,
    w_send, x_recv, s_recv, y_send, y_recv, z_send, z_recv, c_send, c_recv,
):
    group = lax.axis_index("group")
    shard = lax.axis_index("shard")
    col = lax.axis_index("col")
    x, core = group // 2, group % 2
    z, y = shard // 4, shard % 4

    x_peers = [{"group": (x + d) % 4 * 2 + core} for d in (1, 2, 3)]
    y_peers = [{"shard": z * 4 + (y + d) % 4} for d in (1, 2, 3)]
    z_peers = [{"shard": (z + d) % 4 * 4 + y} for d in (1, 2, 3)]
    c_peers = [{"col": (col + d) % 4} for d in (1, 2, 3)]
    sibling = {"group": x * 2 + 1 - core}

    def load(src, dst, sem):
        copy = pltpu.make_async_copy(src, dst, sem)
        copy.start()
        return copy

    barrier = pltpu.get_barrier_semaphore()

    def tell(sem, peer):
        pl.semaphore_signal(sem, inc=1, device_id=peer, device_id_type=MESH)

    for peer in y_peers + x_peers + c_peers:
        tell(barrier, peer)
    for j in (1, 2, 3):
        pl.when(z < j)(functools.partial(tell, barrier, {"shard": j * 4 + y}))
    pl.when(core == 0)(functools.partial(tell, barrier, sibling))

    k_loads = [load(keys_ref.at[0, r], keys.at[r], key_sem.at[r]) for r in range(4)]
    q_load = load(queries_ref, queries, small_sem.at[0])
    l_load = load(lengths_ref, lengths, small_sem.at[1])

    v_load = load(values_ref.at[0], values, value_sem)
    for i, src in enumerate((master_ref, grad_ref, first_ref, second_ref)):
        load(src.at[0], state.at[i], state_sem)
    r_load = load(resident_ref, resident, resident_sem)
    t_load = load(tags_ref, tags, tags_sem)

    def send(src, dst, send_sem, recv_sem, peer):
        pltpu.make_async_remote_copy(
            src_ref=src, dst_ref=dst, send_sem=send_sem, recv_sem=recv_sem, device_id=peer, device_id_type=MESH
        ).start()

    def arrive(ref, sem):
        pltpu.make_async_copy(ref, ref, sem).wait()

    q_load.wait()
    l_load.wait()
    q32 = queries[0].astype(F32)
    tall = [jnp.concatenate([q32[:, h * HS : (h + 1) * HS] for h in range(4 * k, 4 * k + 4)], axis=0) for k in (0, 1)]
    blank = jnp.zeros((16, HS), F32)
    wide = jnp.concatenate(
        [jnp.concatenate([tall[0], blank], axis=1), jnp.concatenate([blank, tall[1]], axis=1)], axis=0
    )
    row_q = lax.broadcasted_iota(jnp.int32, (32, 2 * HS), 0) % 4
    row = lax.broadcasted_iota(jnp.int32, (32, 512), 0) % 4
    position = shard * 512 + lax.broadcasted_iota(jnp.int32, (32, 512), 1)
    limit = jnp.where(
        row == 0, lengths[0, 0], jnp.where(row == 1, lengths[0, 1], jnp.where(row == 2, lengths[0, 2], lengths[0, 3]))
    )
    mask = position < limit
    scores = jnp.zeros((32, 512), F32)
    for r in range(4):
        k_loads[r].wait()
        scores = scores + nt(jnp.where(row_q == r, wide, 0.0).astype(BF16), keys[r])
    scores = scores * (1.0 / HS**0.5)
    best = jnp.max(jnp.where(mask, scores, neg_big), axis=1, keepdims=True)
    best = best.astype(BF16).astype(F32)
    probs = jnp.where(mask, jnp.exp(scores - best), 0.0)
    total = jnp.sum(probs, axis=1, keepdims=True)
    v_load.wait()
    both = jnp.zeros((32, 2 * HS), F32)
    for r in range(4):
        both = both + jnp.dot(
            jnp.where(row == r, probs, 0.0).astype(BF16), values[r], preferred_element_type=F32
        )
    y_out[...] = pack(jnp.concatenate([both[:16, :HS], both[16:, HS:]], axis=0), best, total)

    pl.semaphore_wait(barrier, 9 + z + core)
    for j in (0, 1, 2):
        pl.when(j < z)(functools.partial(tell, z_ready, {"shard": j * 4 + y}))
    pl.when(core == 1)(functools.partial(tell, s_ready, sibling))
    for peer in (y_peers[1], y_peers[0], y_peers[2]):
        send(y_out, y_in.at[y], y_send, y_recv, peer)
    y_in[y] = y_out[...]

    arrive(state, state_sem)
    updated, first_new, second_new = adam(state[0], state[1], state[2], state[3])
    slabs[group] = updated
    for d in (1, 3, 2):
        send(slabs.at[group], slabs.at[group], w_send, x_recv.at[d - 1], x_peers[d - 1])
    updated_ref[0] = updated
    first_out[0] = first_new
    second_out[0] = second_new

    arrive(y_in.at[0:3], y_recv)
    z_out[...] = pack(*merge(y_in))
    pl.when(z < 3)(lambda: pl.semaphore_wait(z_ready, 3 - z))
    for peer in (z_peers[1], z_peers[0], z_peers[2]):
        send(z_out, z_in.at[z], z_send, z_recv, peer)
    z_in[z] = z_out[...]

    pl.when(core == 0)(lambda: pl.semaphore_wait(s_ready, 1))
    send(slabs.at[group], slabs.at[group], w_send, s_recv, sibling)
    for d in (1, 3, 2):
        arrive(slabs.at[0], x_recv.at[d - 1])
        block = (x + 4 - d) % 4 * 2 + core
        send(slabs.at[block], slabs.at[block], w_send, s_recv, sibling)
    r_load.wait()
    t_load.wait()
    odd = jnp.full((320, HS), tags[0], jnp.int32) % 2 == 1
    arrive(slabs.at[0:4], s_recv)
    for h in range(8):
        place = (h % 2 * 4 + h // 2) * HS
        chosen[:, place : place + HS] = jnp.where(odd, slabs[h], resident[0, :, h * HS : (h + 1) * HS])

    arrive(z_in.at[0:3], z_recv)
    acc, _, total = merge(z_in)
    acc = acc / total
    attended = jnp.concatenate([acc[8 * j : 8 * j + 8] for j in range(4)], axis=1).astype(BF16)
    even = nt(attended, chosen[:, : 4 * HS])
    uneven = nt(attended, chosen[:, 4 * HS :])
    share = even[:4] + uneven[4:]
    c_in[col] = jnp.concatenate(
        [
            share[:, :HS],
            share[:, HS : 2 * HS],
            jnp.concatenate([share[:, 2 * HS :], jnp.zeros((4, 64), F32)], axis=1),
            jnp.zeros((4, HS), F32),
        ],
        axis=0,
    ).astype(BF16)
    for peer in (c_peers[2], c_peers[1], c_peers[0]):
        send(c_in.at[col], c_in.at[col], c_send, c_recv, peer)
    arrive(c_in.at[0:3], c_recv)
    final = c_in[0].astype(F32) + c_in[1].astype(F32) + c_in[2].astype(F32) + c_in[3].astype(F32)
    out_ref[0] = jnp.concatenate([final[0:4], final[4:8], final[8:12, :64]], axis=1).astype(BF16)
    arrive(y_in.at[0:3], y_send)
    arrive(z_in.at[0:3], z_send)
    arrive(c_in.at[0:3], c_send)
    arrive(slabs.at[0:7], w_send)


def writer(*refs):
    sems = refs[-1]
    copies = [pltpu.make_async_copy(refs[i], refs[4 + i], sems.at[i]) for i in range(4)]
    for copy in copies:
        copy.start()
    for copy in copies:
        copy.wait()


def per_device(master, grad, first, second, resident, tags, queries, keys, values, lengths):
    flip = functools.partial(jnp.swapaxes, axis1=1, axis2=2)
    dma = pltpu.SemaphoreType.DMA
    rows, width = queries.shape[1], master.shape[2]
    shapes = [(1, width, HS)] * 3 + [(1, rows, width)]
    operands = (
        flip(master), flip(grad), flip(first), flip(second), flip(resident), tags, queries, keys, values, lengths
    )
    held = pl.pallas_call(
        kernel,
        out_shape=[pltpu.VMEM(shape, BF16) for shape in shapes],
        in_specs=[pl.BlockSpec(memory_space=pltpu.HBM)] * 10,
        out_specs=[pl.BlockSpec(memory_space=pltpu.VMEM)] * 4,
        scratch_shapes=[
            pltpu.VMEM((4, 320, 128), BF16),
            pltpu.VMEM((1, 320, 1024), BF16),
            pltpu.SMEM((1,), jnp.int32),
            pltpu.VMEM((1, 4, 1024), BF16),
            pltpu.VMEM((4, 512, 256), BF16),
            pltpu.VMEM((4, 512, 256), BF16),
            pltpu.SMEM((1, 4), jnp.int32),
            pltpu.VMEM((8, 320, 128), BF16),
            pltpu.VMEM((320, 1024), BF16),
            pltpu.VMEM((48, 128), BF16),
            pltpu.VMEM((4, 48, 128), BF16),
            pltpu.VMEM((48, 128), BF16),
            pltpu.VMEM((4, 48, 128), BF16),
            pltpu.VMEM((4, 16, 128), BF16),
            pltpu.SemaphoreType.REGULAR, pltpu.SemaphoreType.REGULAR,
            dma((2,)), dma((4,)), dma, dma, dma, dma,
            dma, dma((3,)), dma, dma, dma, dma, dma, dma, dma,
        ],
        compiler_params=pltpu.CompilerParams(collective_id=0, has_side_effects=True),
    )(
        *[value if value is tags else pltpu.with_memory_space_constraint(value, pltpu.HBM) for value in operands]
    )
    updated, first_new, second_new, projected = pl.pallas_call(
        writer,
        out_shape=[pltpu.HBM(shape, BF16) for shape in shapes],
        in_specs=[pl.BlockSpec(memory_space=pltpu.VMEM)] * 4,
        out_specs=[pl.BlockSpec(memory_space=pltpu.HBM)] * 4,
        scratch_shapes=[dma((4,))],
    )(*[pltpu.with_memory_space_constraint(value, pltpu.VMEM) for value in held])
    return flip(updated), flip(first_new), flip(second_new), projected


def solution(mesh):
    return jax.shard_map(
        per_device,
        mesh=mesh,
        in_specs=(
            P("col", "group", "shard"),
            P("col", "group", "shard"),
            P("col", "group", "shard"),
            P("col", "group", "shard"),
            P("group", "col", "shard"),
            P("group"),
            P("group", None, "col"),
            P("group", None, "shard", "col"),
            P("group", None, "shard", "col"),
            P("group", None),
        ),
        out_specs=(
            P("col", "group", "shard"),
            P("col", "group", "shard"),
            P("col", "group", "shard"),
            P("group", None, "shard"),
        ),
        check_vma=False,
    )
```

time: 36.7 us -> 30.2 us (0.82)
  Pallas kernels: 33 us -> 28.8 us
  local copies, waits for them, and re-layouts: 1.28 us -> 0 us
  other arithmetic: 0.87 us -> 0 us
    pallas_call x1 -> x2, Pallas kernels: 33 us -> 28.8 us  [the longest x1 28 us: per_device(): pl.pallas_call(kernel, out_shape=[pltpu.VMEM(shape, BF16) for shape in sh...]
    unnamed x11 -> x0, local copies, waits for them, and re-layouts: 1.28 us -> none
    convert_element_type x1 -> x0, other arithmetic: 0.87 us -> none  [adam(): second_new.astype(BF16)]
where the time goes in v2:
time: 30.2 us; the launch traced here: 30 us
  Pallas kernels  28.8 us (95%)
  between operations  1.29 us (4%)
    pallas_call x1, Pallas kernels, per_device(): pl.pallas_call(kernel, out_shape=[pltpu.VMEM(shape, BF16) for shape in sh...  28 us
    pallas_call x1, Pallas kernels, per_device(): pl.pallas_call(writer, out_shape=[pltpu.HBM(shape, BF16) for shape in sha...  0.73 us

profile of v2, /device:TPU:6, one launch (start us, length us, event | category | flops | bytes accessed | tf_op | source)
XLA Modules:
  0.0 30.0 jit_solution(4112230335980198077)
XLA Ops:
  1.3 28.0 %shard_map.129 = (bf16[1,320,128]{2,1,0:T(8,128)(2,1)S(1)}, bf16[1,320,128]{2,1,0:T(8,128)(2,1)S(1)}, bf16[1,320,128]{2,1,0:T(8,128)(2,1)S(1)}, bf16[1,4,320]{2,1,0:T(4,128)(2,1)S(1)}) custom-call(bf16[1,320,128]{2,1,0:T(8,128)(2,1)} %bitcast.9, bf16[1,320,128]{2,1,0:T(8,128)(2,1)} %bitcast.10, bf16[1,320,128]{2,1,0:T(8,128)(2,1)} %bitcast.11, ...), custom_call_target="tpu_custom_call" | custom-call | tf_op jit(solution)/shard_map/pallas_call | solution.py:232
  29.3 0.7 %shard_map.130 = (bf16[1,320,128]{2,1,0:T(8,128)(2,1)}, bf16[1,320,128]{2,1,0:T(8,128)(2,1)}, bf16[1,320,128]{2,1,0:T(8,128)(2,1)}, bf16[1,4,320]{2,1,0:T(4,128)(2,1)}) custom-call(bf16[1,320,128]{2,1,0:T(8,128)(2,1)S(1)} %get-tuple-element.12.refs_0_, bf16[1,320,128]{2,1,0:T(8,128)(2,1)S(1)} %get-tuple-element.13.refs_1_, ...), custom_call_target="tpu_custom_call" | custom-call | tf_op jit(solution)/shard_map/pallas_call | solution.py:260

commit v3 on v2

--- a/solution.py
+++ b/solution.py
@@ -22,6 +22,10 @@
 neg_big = -1e30
 
 
+def chosen_row(row):
+    return row < 2
+
+
 def adam(master, grad, first, second):
     g32 = grad.astype(F32)
     first_new = beta_one * first.astype(F32) + (1.0 - beta_one) * g32
@@ -38,36 +42,31 @@
     return lax.dot_general(a, b, (((1,), (1,)), ((), ())), preferred_element_type=F32)
 
 
-def pack(acc, best, total):
-    lane = lax.broadcasted_iota(jnp.int32, (16, HS), 1)
-    high = total.astype(BF16).astype(F32)
-    low = total - high
-    stats = jnp.zeros((16, HS), F32)
-    for i, column in enumerate((best[:16], high[:16], low[:16], best[16:], high[16:], low[16:])):
-        stats = jnp.where(lane == i, column, stats)
-    return jnp.concatenate([acc, stats], axis=0).astype(BF16)
-
-
-def merge(shares):
-    parts = [shares[i].astype(F32) for i in range(4)]
-    bests = [jnp.concatenate([part[32:, 0:1], part[32:, 3:4]], axis=0) for part in parts]
-    best = jnp.maximum(jnp.maximum(bests[0], bests[1]), jnp.maximum(bests[2], bests[3]))
-    acc, total = 0.0, 0.0
-    for part, own in zip(parts, bests):
-        factor = jnp.exp(own - best)
-        acc = acc + part[:32] * factor
-        sums = jnp.concatenate([part[32:, 1:2] + part[32:, 2:3], part[32:, 4:5] + part[32:, 5:6]], axis=0)
-        total = total + sums * factor
-    return acc, best, total
+def pack(best, total):
+    lane = lax.broadcasted_iota(jnp.int32, (32, HS), 1)
+    stats = jnp.where(lane == 0, best, jnp.where(lane == 1, total, 0.0)).T[:2]
+    return jnp.concatenate([stats, jnp.zeros((2, HS - 32), F32)], axis=1)
+
+
+def merge(shares, last=False):
+    best = functools.reduce(jnp.maximum, [stats[0:1] for _, stats in shares])
+    factors = [jnp.exp(stats[0:1] - best) for _, stats in shares]
+    total = sum(stats[1:2] * factor for (_, stats), factor in zip(shares, factors))
+    if last:
+        factors = [factor / total for factor in factors]
+    blank = jnp.zeros((8 - len(shares), HS), F32)
+    columns = jnp.concatenate(factors + [blank], axis=0).T[:32]
+    acc = sum(rows.astype(F32) * columns[:, i : i + 1] for i, (rows, _) in enumerate(shares))
+    return acc, jnp.concatenate([best, total], axis=0)
 
 
 def kernel(
     master_ref, grad_ref, first_ref, second_ref, resident_ref, tags_ref, queries_ref, keys_ref, values_ref, lengths_ref,
     updated_ref, first_out, second_out, out_ref,
     state, resident, tags, queries, keys, values, lengths,
-    slabs, chosen, y_out, y_in, z_out, z_in, c_in,
+    slabs, chosen, y_out, y_in, z_out, z_in, d_in, y_top, y_tops, z_top, z_tops, d_tops, attended, c_in,
     z_ready, s_ready, small_sem, key_sem, value_sem, state_sem, resident_sem, tags_sem,
-    w_send, x_recv, s_recv, y_send, y_recv, z_send, z_recv, c_send, c_recv,
+    w_send, x_recv, s_recv, y_send, y_recv, z_send, z_recv, d_send, d_recv, e_recv, c_send, c_recv,
 ):
     group = lax.axis_index("group")
     shard = lax.axis_index("shard")
@@ -86,6 +85,9 @@
         copy.start()
         return copy
 
+    q_load = load(queries_ref, queries, small_sem.at[0])
+    l_load = load(lengths_ref, lengths, small_sem.at[1])
+    k_loads = [load(keys_ref.at[0, r], keys.at[r], key_sem.at[r]) for r in range(4)]
     barrier = pltpu.get_barrier_semaphore()
 
     def tell(sem, peer):
@@ -93,19 +95,22 @@
 
     for peer in y_peers + x_peers + c_peers:
         tell(barrier, peer)
-    for j in (1, 2, 3):
-        pl.when(z < j)(functools.partial(tell, barrier, {"shard": j * 4 + y}))
+    def tell_late():
+        for j in (3, 2):
+            for i in range(4):
+                tell(barrier, {"shard": j * 4 + i})
+        tell(barrier, {"shard": 4 + y})
+
+    chosen_y = chosen_row(y)
+    first = (z == 0) & chosen_y
+    late = z > 1
+    pl.when(first)(tell_late)
+    for j in (3, 2):
+        pl.when(jnp.logical_not(first) & (z < j))(functools.partial(tell, barrier, {"shard": j * 4 + y}))
+    pl.when(jnp.logical_not(first) & (z < 1))(functools.partial(tell, barrier, {"shard": 4 + y}))
     pl.when(core == 0)(functools.partial(tell, barrier, sibling))
 
-    k_loads = [load(keys_ref.at[0, r], keys.at[r], key_sem.at[r]) for r in range(4)]
-    q_load = load(queries_ref, queries, small_sem.at[0])
-    l_load = load(lengths_ref, lengths, small_sem.at[1])
-
-    v_load = load(values_ref.at[0], values, value_sem)
-    for i, src in enumerate((master_ref, grad_ref, first_ref, second_ref)):
-        load(src.at[0], state.at[i], state_sem)
-    r_load = load(resident_ref, resident, resident_sem)
-    t_load = load(tags_ref, tags, tags_sem)
+    v_loads = [load(values_ref.at[0, r], values.at[r], value_sem.at[r]) for r in range(4)]
 
     def send(src, dst, send_sem, recv_sem, peer):
         pltpu.make_async_remote_copy(
@@ -116,7 +121,6 @@
         pltpu.make_async_copy(ref, ref, sem).wait()
 
     q_load.wait()
-    l_load.wait()
     q32 = queries[0].astype(F32)
     tall = [jnp.concatenate([q32[:, h * HS : (h + 1) * HS] for h in range(4 * k, 4 * k + 4)], axis=0) for k in (0, 1)]
     blank = jnp.zeros((16, HS), F32)
@@ -125,35 +129,55 @@
     )
     row_q = lax.broadcasted_iota(jnp.int32, (32, 2 * HS), 0) % 4
     row = lax.broadcasted_iota(jnp.int32, (32, 512), 0) % 4
-    position = shard * 512 + lax.broadcasted_iota(jnp.int32, (32, 512), 1)
-    limit = jnp.where(
-        row == 0, lengths[0, 0], jnp.where(row == 1, lengths[0, 1], jnp.where(row == 2, lengths[0, 2], lengths[0, 3]))
-    )
-    mask = position < limit
     scores = jnp.zeros((32, 512), F32)
     for r in range(4):
         k_loads[r].wait()
         scores = scores + nt(jnp.where(row_q == r, wide, 0.0).astype(BF16), keys[r])
+    for i, src in enumerate((master_ref, grad_ref, first_ref, second_ref)):
+        load(src.at[0], state.at[i], state_sem)
+    r_load = load(resident_ref, resident, resident_sem)
+    t_load = load(tags_ref, tags, tags_sem)
+
+    l_load.wait()
+    for copy in v_loads:
+        copy.wait()
+    position = shard * 512 + lax.broadcasted_iota(jnp.int32, (32, 512), 1)
+    limit = jnp.where(
+        row == 0, lengths[0, 0], jnp.where(row == 1, lengths[0, 1], jnp.where(row == 2, lengths[0, 2], lengths[0, 3]))
+    )
+    mask = position < limit
     scores = scores * (1.0 / HS**0.5)
     best = jnp.max(jnp.where(mask, scores, neg_big), axis=1, keepdims=True)
-    best = best.astype(BF16).astype(F32)
     probs = jnp.where(mask, jnp.exp(scores - best), 0.0)
     total = jnp.sum(probs, axis=1, keepdims=True)
-    v_load.wait()
     both = jnp.zeros((32, 2 * HS), F32)
     for r in range(4):
         both = both + jnp.dot(
             jnp.where(row == r, probs, 0.0).astype(BF16), values[r], preferred_element_type=F32
         )
-    y_out[...] = pack(jnp.concatenate([both[:16, :HS], both[16:, HS:]], axis=0), best, total)
-
-    pl.semaphore_wait(barrier, 9 + z + core)
+    y_out[...] = jnp.concatenate([both[:16, :HS], both[16:, HS:]], axis=0).astype(BF16)
+    y_top[...] = pack(best, total)
+
+    several = sum(jnp.where(chosen_row(i), 1, 0) for i in range(4))
+    pl.semaphore_wait(barrier, 9 + z + core + jnp.where(late, several - jnp.where(chosen_y, 1, 0), 0))
+
+    def send_direct():
+        def send_one(i, place):
+            send(y_out, d_in.at[place], d_send.at[0], d_recv.at[z - 2], {"shard": i})
+            send(y_top, d_tops.at[place], d_send.at[1], e_recv.at[z - 2], {"shard": i})
+
+        for i in range(4):
+            pl.when(chosen_row(i))(functools.partial(send_one, i, (z - 2) * 4 + y))
+
+    pl.when(late)(send_direct)
+    for peer in (y_peers[1], y_peers[0], y_peers[2]):
+        send(y_out, y_in.at[y], y_send.at[0], y_recv.at[0], peer)
+        send(y_top, y_tops.at[y], y_send.at[1], y_recv.at[1], peer)
     for j in (0, 1, 2):
         pl.when(j < z)(functools.partial(tell, z_ready, {"shard": j * 4 + y}))
     pl.when(core == 1)(functools.partial(tell, s_ready, sibling))
-    for peer in (y_peers[1], y_peers[0], y_peers[2]):
-        send(y_out, y_in.at[y], y_send, y_recv, peer)
     y_in[y] = y_out[...]
+    y_tops[y] = y_top[...]
 
     arrive(state, state_sem)
     updated, first_new, second_new = adam(state[0], state[1], state[2], state[3])
@@ -164,19 +188,37 @@
     first_out[0] = first_new
     second_out[0] = second_new
 
-    arrive(y_in.at[0:3], y_recv)
-    z_out[...] = pack(*merge(y_in))
-    pl.when(z < 3)(lambda: pl.semaphore_wait(z_ready, 3 - z))
-    for peer in (z_peers[1], z_peers[0], z_peers[2]):
-        send(z_out, z_in.at[z], z_send, z_recv, peer)
+    arrive(y_in.at[0:3], y_recv.at[0])
+    arrive(y_tops.at[0:3], y_recv.at[1])
+    rows, top = merge([(y_in[i], y_tops[i]) for i in range(4)])
+    z_out[...] = rows.astype(BF16)
+    z_top[...] = top
+    def send_z(j):
+        send(z_out, z_in.at[z], z_send.at[0], z_recv.at[0], {"shard": j * 4 + y})
+        send(z_top, z_tops.at[z], z_send.at[1], z_recv.at[1], {"shard": j * 4 + y})
+
+    pl.when((z == 1) | late & jnp.logical_not(chosen_y))(functools.partial(send_z, 0))
+    for j in (1, 2):
+        pl.when(j < z)(functools.partial(send_z, j))
     z_in[z] = z_out[...]
-
-    pl.when(core == 0)(lambda: pl.semaphore_wait(s_ready, 1))
-    send(slabs.at[group], slabs.at[group], w_send, s_recv, sibling)
-    for d in (1, 3, 2):
-        arrive(slabs.at[0], x_recv.at[d - 1])
-        block = (x + 4 - d) % 4 * 2 + core
-        send(slabs.at[block], slabs.at[block], w_send, s_recv, sibling)
+    z_tops[z] = z_top[...]
+
+    def pass_on():
+        pl.when(core == 0)(lambda: pl.semaphore_wait(s_ready, 1))
+        send(slabs.at[group], slabs.at[group], w_send, s_recv, sibling)
+        for d in (1, 3, 2):
+            arrive(slabs.at[0], x_recv.at[d - 1])
+            block = (x + 4 - d) % 4 * 2 + core
+            send(slabs.at[block], slabs.at[block], w_send, s_recv, sibling)
+
+    def send_later():
+        pl.semaphore_wait(z_ready, 3 - z)
+        for j in (3, 2, 1):
+            pl.when(j > z)(functools.partial(send_z, j))
+
+    pl.when(z < 2)(pass_on)
+    pl.when(z < 3)(send_later)
+    pl.when(z >= 2)(pass_on)
     r_load.wait()
     t_load.wait()
     odd = jnp.full((320, HS), tags[0], jnp.int32) % 2 == 1
@@ -185,12 +227,29 @@
         place = (h % 2 * 4 + h // 2) * HS
         chosen[:, place : place + HS] = jnp.where(odd, slabs[h], resident[0, :, h * HS : (h + 1) * HS])
 
-    arrive(z_in.at[0:3], z_recv)
-    acc, _, total = merge(z_in)
-    acc = acc / total
-    attended = jnp.concatenate([acc[8 * j : 8 * j + 8] for j in range(4)], axis=1).astype(BF16)
-    even = nt(attended, chosen[:, : 4 * HS])
-    uneven = nt(attended, chosen[:, 4 * HS :])
+    def finish(shares):
+        acc, _ = merge(shares, last=True)
+        attended[...] = jnp.concatenate([acc[8 * j : 8 * j + 8] for j in range(4)], axis=1).astype(BF16)
+
+    def finish_first():
+        arrive(z_in.at[0], z_recv.at[0])
+        arrive(z_tops.at[0], z_recv.at[1])
+        arrive(d_in.at[0:4], d_recv.at[1])
+        arrive(d_tops.at[0:4], e_recv.at[1])
+        running = merge([(z_in[i], z_tops[i]) for i in (0, 1)] + [(d_in[i], d_tops[i]) for i in (4, 5, 6, 7)])
+        arrive(d_in.at[0:4], d_recv.at[0])
+        arrive(d_tops.at[0:4], e_recv.at[0])
+        finish([running] + [(d_in[i], d_tops[i]) for i in (0, 1, 2, 3)])
+
+    def finish_other():
+        arrive(z_in.at[0:3], z_recv.at[0])
+        arrive(z_tops.at[0:3], z_recv.at[1])
+        finish([(z_in[i], z_tops[i]) for i in range(4)])
+
+    pl.when(first)(finish_first)
+    pl.when(jnp.logical_not(first))(finish_other)
+    even = nt(attended[...], chosen[:, : 4 * HS])
+    uneven = nt(attended[...], chosen[:, 4 * HS :])
     share = even[:4] + uneven[4:]
     c_in[col] = jnp.concatenate(
         [
@@ -206,8 +265,22 @@
     arrive(c_in.at[0:3], c_recv)
     final = c_in[0].astype(F32) + c_in[1].astype(F32) + c_in[2].astype(F32) + c_in[3].astype(F32)
     out_ref[0] = jnp.concatenate([final[0:4], final[4:8], final[8:12, :64]], axis=1).astype(BF16)
-    arrive(y_in.at[0:3], y_send)
-    arrive(z_in.at[0:3], z_send)
+    arrive(y_in.at[0:3], y_send.at[0])
+    arrive(y_tops.at[0:3], y_send.at[1])
+    fewer = late & chosen_y
+
+    def sent(count):
+        arrive(z_in.at[0:count], z_send.at[0])
+        arrive(z_tops.at[0:count], z_send.at[1])
+
+    def sent_direct():
+        arrive(d_in.at[0], d_send.at[0])
+        arrive(d_tops.at[0], d_send.at[1])
+
+    pl.when(jnp.logical_not(fewer))(functools.partial(sent, 3))
+    pl.when(fewer)(functools.partial(sent, 2))
+    for i in range(4):
+        pl.when(late & chosen_row(i))(sent_direct)
     arrive(c_in.at[0:3], c_send)
     arrive(slabs.at[0:7], w_send)
 
@@ -244,14 +317,21 @@
             pltpu.SMEM((1, 4), jnp.int32),
             pltpu.VMEM((8, 320, 128), BF16),
             pltpu.VMEM((320, 1024), BF16),
-            pltpu.VMEM((48, 128), BF16),
-            pltpu.VMEM((4, 48, 128), BF16),
-            pltpu.VMEM((48, 128), BF16),
-            pltpu.VMEM((4, 48, 128), BF16),
+            pltpu.VMEM((32, 128), BF16),
+            pltpu.VMEM((4, 32, 128), BF16),
+            pltpu.VMEM((32, 128), BF16),
+            pltpu.VMEM((4, 32, 128), BF16),
+            pltpu.VMEM((8, 32, 128), BF16),
+            pltpu.VMEM((2, 128), F32),
+            pltpu.VMEM((4, 2, 128), F32),
+            pltpu.VMEM((2, 128), F32),
+            pltpu.VMEM((4, 2, 128), F32),
+            pltpu.VMEM((8, 2, 128), F32),
+            pltpu.VMEM((8, 512), BF16),
             pltpu.VMEM((4, 16, 128), BF16),
             pltpu.SemaphoreType.REGULAR, pltpu.SemaphoreType.REGULAR,
-            dma((2,)), dma((4,)), dma, dma, dma, dma,
-            dma, dma((3,)), dma, dma, dma, dma, dma, dma, dma,
+            dma((2,)), dma((4,)), dma((4,)), dma, dma, dma,
+            dma, dma((3,)), dma, dma((2,)), dma((2,)), dma((2,)), dma((2,)), dma((2,)), dma((2,)), dma((2,)), dma, dma,
         ],
         compiler_params=pltpu.CompilerParams(collective_id=0, has_side_effects=True),
     )(

time: 30.2 us -> 29.3 us (0.970)
  the two profiles are of different devices: /device:TPU:6 before, /device:TPU:16 now
where the time goes in v3:
time: 29.3 us; the launch traced here: 29.1 us
  Pallas kernels  27.8 us (95%)
  between operations  1.29 us (4%)
    pallas_call x1, Pallas kernels, per_device(): pl.pallas_call(kernel, out_shape=[pltpu.VMEM(shape, BF16) for shape in sh...  27.1 us
    pallas_call x1, Pallas kernels, per_device(): pl.pallas_call(writer, out_shape=[pltpu.HBM(shape, BF16) for shape in sha...  0.73 us

profile of v3, /device:TPU:16, one launch (start us, length us, event | category | flops | bytes accessed | tf_op | source)
XLA Modules:
  0.0 29.1 jit_solution(6815881241928191638)
XLA Ops:
  1.3 27.1 %shard_map.129 = (bf16[1,320,128]{2,1,0:T(8,128)(2,1)S(1)}, bf16[1,320,128]{2,1,0:T(8,128)(2,1)S(1)}, bf16[1,320,128]{2,1,0:T(8,128)(2,1)S(1)}, bf16[1,4,320]{2,1,0:T(4,128)(2,1)S(1)}) custom-call(bf16[1,320,128]{2,1,0:T(8,128)(2,1)} %bitcast.9, bf16[1,320,128]{2,1,0:T(8,128)(2,1)} %bitcast.10, bf16[1,320,128]{2,1,0:T(8,128)(2,1)} %bitcast.11, ...), custom_call_target="tpu_custom_call" | custom-call | tf_op jit(solution)/shard_map/pallas_call | solution.py:305
  28.4 0.7 %shard_map.130 = (bf16[1,320,128]{2,1,0:T(8,128)(2,1)}, bf16[1,320,128]{2,1,0:T(8,128)(2,1)}, bf16[1,320,128]{2,1,0:T(8,128)(2,1)}, bf16[1,4,320]{2,1,0:T(4,128)(2,1)}) custom-call(bf16[1,320,128]{2,1,0:T(8,128)(2,1)S(1)} %get-tuple-element.12.refs_0_, bf16[1,320,128]{2,1,0:T(8,128)(2,1)S(1)} %get-tuple-element.13.refs_1_, ...), custom_call_target="tpu_custom_call" | custom-call | tf_op jit(solution)/shard_map/pallas_call | solution.py:340

commit v4 on v3

--- a/solution.py
+++ b/solution.py
@@ -20,10 +20,6 @@
 correct_one = 1.0
 correct_two = 0.6323045752
 neg_big = -1e30
-
-
-def chosen_row(row):
-    return row < 2
 
 
 def adam(master, grad, first, second):
@@ -65,8 +61,8 @@
     updated_ref, first_out, second_out, out_ref,
     state, resident, tags, queries, keys, values, lengths,
     slabs, chosen, y_out, y_in, z_out, z_in, d_in, y_top, y_tops, z_top, z_tops, d_tops, attended, c_in,
-    z_ready, s_ready, small_sem, key_sem, value_sem, state_sem, resident_sem, tags_sem,
-    w_send, x_recv, s_recv, y_send, y_recv, z_send, z_recv, d_send, d_recv, e_recv, c_send, c_recv,
+    z_ready, s_ready, c_ready, small_sem, key_sem, value_sem, state_sem, resident_sem, tags_sem,
+    w_send, x_recv, s_recv, y_send, y_recv, z_send, z_recv, d_send, d_recv, c_send, c_recv,
 ):
     group = lax.axis_index("group")
     shard = lax.axis_index("shard")
@@ -93,22 +89,23 @@
     def tell(sem, peer):
         pl.semaphore_signal(sem, inc=1, device_id=peer, device_id_type=MESH)
 
-    for peer in y_peers + x_peers + c_peers:
+    for peer in y_peers + x_peers:
         tell(barrier, peer)
-    def tell_late():
-        for j in (3, 2):
-            for i in range(4):
-                tell(barrier, {"shard": j * 4 + i})
-        tell(barrier, {"shard": 4 + y})
-
-    chosen_y = chosen_row(y)
-    first = (z == 0) & chosen_y
-    late = z > 1
-    pl.when(first)(tell_late)
-    for j in (3, 2):
-        pl.when(jnp.logical_not(first) & (z < j))(functools.partial(tell, barrier, {"shard": j * 4 + y}))
-    pl.when(jnp.logical_not(first) & (z < 1))(functools.partial(tell, barrier, {"shard": 4 + y}))
+    first, late = z == 0, z == 2
+
+    def tell_first():
+        for i in range(4):
+            tell(barrier, {"shard": 8 + i})
+
+    pl.when(first)(tell_first)
+    pl.when(z == 1)(functools.partial(tell, barrier, {"shard": 8 + y}))
+    for j in (3, 1):
+        pl.when(z == 0)(functools.partial(tell, barrier, {"shard": 4 * j + y}))
     pl.when(core == 0)(functools.partial(tell, barrier, sibling))
+    before = jnp.where(z == 3, 3 - col, col)
+    for d in (1, 2, 3):
+        peer = {"col": jnp.where(z == 3, 3 - before - d, before + d)}
+        pl.when(before + d < 4)(functools.partial(tell, barrier, peer))
 
     v_loads = [load(values_ref.at[0, r], values.at[r], value_sem.at[r]) for r in range(4)]
 
@@ -158,24 +155,28 @@
     y_out[...] = jnp.concatenate([both[:16, :HS], both[16:, HS:]], axis=0).astype(BF16)
     y_top[...] = pack(best, total)
 
-    several = sum(jnp.where(chosen_row(i), 1, 0) for i in range(4))
-    pl.semaphore_wait(barrier, 9 + z + core + jnp.where(late, several - jnp.where(chosen_y, 1, 0), 0))
+    told = jnp.where(late, 5, jnp.where(first, 0, 1))
+    pl.semaphore_wait(barrier, 6 + core + told + before)
 
     def send_direct():
         def send_one(i, place):
-            send(y_out, d_in.at[place], d_send.at[0], d_recv.at[z - 2], {"shard": i})
-            send(y_top, d_tops.at[place], d_send.at[1], e_recv.at[z - 2], {"shard": i})
+            send(y_out, d_in.at[place], d_send.at[0], d_recv.at[0], {"shard": i})
+            send(y_top, d_tops.at[place], d_send.at[1], d_recv.at[1], {"shard": i})
 
         for i in range(4):
-            pl.when(chosen_row(i))(functools.partial(send_one, i, (z - 2) * 4 + y))
+            send_one(i, y)
 
     pl.when(late)(send_direct)
-    for peer in (y_peers[1], y_peers[0], y_peers[2]):
+    for peer in ({"shard": z * 4 + i} for i in (y + 1 - y % 2 * 2, (y + 2) % 4, 3 - y)):
         send(y_out, y_in.at[y], y_send.at[0], y_recv.at[0], peer)
         send(y_top, y_tops.at[y], y_send.at[1], y_recv.at[1], peer)
-    for j in (0, 1, 2):
-        pl.when(j < z)(functools.partial(tell, z_ready, {"shard": j * 4 + y}))
+    for j in (1, 2, 3):
+        pl.when(z == j)(functools.partial(tell, z_ready.at[j], {"shard": y}))
+    pl.when(late)(functools.partial(tell, z_ready.at[2], {"shard": 4 + y}))
     pl.when(core == 1)(functools.partial(tell, s_ready, sibling))
+    for d in (1, 2, 3):
+        peer = {"col": jnp.where(z == 3, 3 - before + d, before - d)}
+        pl.when(before >= d)(functools.partial(tell, c_ready, peer))
     y_in[y] = y_out[...]
     y_tops[y] = y_top[...]
 
@@ -197,9 +198,17 @@
         send(z_out, z_in.at[z], z_send.at[0], z_recv.at[0], {"shard": j * 4 + y})
         send(z_top, z_tops.at[z], z_send.at[1], z_recv.at[1], {"shard": j * 4 + y})
 
-    pl.when((z == 1) | late & jnp.logical_not(chosen_y))(functools.partial(send_z, 0))
-    for j in (1, 2):
-        pl.when(j < z)(functools.partial(send_z, j))
+    def heard(j):
+        pl.semaphore_wait(z_ready.at[j], 1)
+
+    pl.when((z == 1) | (z == 3))(functools.partial(send_z, 0))
+    pl.when(late)(functools.partial(send_z, 1))
+
+    def block_three():
+        heard(1)
+        send_z(1)
+
+    pl.when(z == 3)(block_three)
     z_in[z] = z_out[...]
     z_tops[z] = z_top[...]
 
@@ -211,14 +220,35 @@
             block = (x + 4 - d) % 4 * 2 + core
             send(slabs.at[block], slabs.at[block], w_send, s_recv, sibling)
 
-    def send_later():
-        pl.semaphore_wait(z_ready, 3 - z)
-        for j in (3, 2, 1):
-            pl.when(j > z)(functools.partial(send_z, j))
-
-    pl.when(z < 2)(pass_on)
-    pl.when(z < 3)(send_later)
-    pl.when(z >= 2)(pass_on)
+    def block_zero():
+        heard(1)
+        send_z(1)
+        heard(3)
+        tell(z_ready.at[1], {"shard": 12 + y})
+        tell(z_ready.at[3], {"shard": 4 + y})
+        send_z(3)
+        heard(2)
+        tell(z_ready.at[2], {"shard": 12 + y})
+        tell(z_ready.at[3], {"shard": 8 + y})
+        send_z(2)
+
+    def block_one():
+        heard(2)
+        send_z(2)
+        heard(3)
+        send_z(3)
+
+    def block_two():
+        heard(3)
+        send_z(3)
+
+    def block_three_late():
+        heard(2)
+        send_z(2)
+
+    pass_on()
+    for j, step in enumerate((block_zero, block_one, block_two, block_three_late)):
+        pl.when(z == j)(step)
     r_load.wait()
     t_load.wait()
     odd = jnp.full((320, HS), tags[0], jnp.int32) % 2 == 1
@@ -232,20 +262,19 @@
         attended[...] = jnp.concatenate([acc[8 * j : 8 * j + 8] for j in range(4)], axis=1).astype(BF16)
 
     def finish_first():
-        arrive(z_in.at[0], z_recv.at[0])
-        arrive(z_tops.at[0], z_recv.at[1])
-        arrive(d_in.at[0:4], d_recv.at[1])
-        arrive(d_tops.at[0:4], e_recv.at[1])
-        running = merge([(z_in[i], z_tops[i]) for i in (0, 1)] + [(d_in[i], d_tops[i]) for i in (4, 5, 6, 7)])
-        arrive(d_in.at[0:4], d_recv.at[0])
-        arrive(d_tops.at[0:4], e_recv.at[0])
-        finish([running] + [(d_in[i], d_tops[i]) for i in (0, 1, 2, 3)])
+        arrive(z_in.at[0:2], z_recv.at[0])
+        arrive(z_tops.at[0:2], z_recv.at[1])
+        running = merge([(z_in[i], z_tops[i]) for i in (0, 1, 3)])
+        arrive(d_in, d_recv.at[0])
+        arrive(d_tops, d_recv.at[1])
+        finish([running] + [(d_in[i], d_tops[i]) for i in range(4)])
 
     def finish_other():
         arrive(z_in.at[0:3], z_recv.at[0])
         arrive(z_tops.at[0:3], z_recv.at[1])
         finish([(z_in[i], z_tops[i]) for i in range(4)])
 
+    pl.when(before < 3)(lambda: pl.semaphore_wait(c_ready, 3 - before))
     pl.when(first)(finish_first)
     pl.when(jnp.logical_not(first))(finish_other)
     even = nt(attended[...], chosen[:, : 4 * HS])
@@ -267,20 +296,18 @@
     out_ref[0] = jnp.concatenate([final[0:4], final[4:8], final[8:12, :64]], axis=1).astype(BF16)
     arrive(y_in.at[0:3], y_send.at[0])
     arrive(y_tops.at[0:3], y_send.at[1])
-    fewer = late & chosen_y
 
     def sent(count):
         arrive(z_in.at[0:count], z_send.at[0])
         arrive(z_tops.at[0:count], z_send.at[1])
 
     def sent_direct():
-        arrive(d_in.at[0], d_send.at[0])
-        arrive(d_tops.at[0], d_send.at[1])
-
-    pl.when(jnp.logical_not(fewer))(functools.partial(sent, 3))
-    pl.when(fewer)(functools.partial(sent, 2))
-    for i in range(4):
-        pl.when(late & chosen_row(i))(sent_direct)
+        arrive(d_in, d_send.at[0])
+        arrive(d_tops, d_send.at[1])
+
+    pl.when(z != 2)(functools.partial(sent, 3))
+    pl.when(late)(functools.partial(sent, 2))
+    pl.when(late)(sent_direct)
     arrive(c_in.at[0:3], c_send)
     arrive(slabs.at[0:7], w_send)
 
@@ -321,17 +348,17 @@
             pltpu.VMEM((4, 32, 128), BF16),
             pltpu.VMEM((32, 128), BF16),
             pltpu.VMEM((4, 32, 128), BF16),
-            pltpu.VMEM((8, 32, 128), BF16),
+            pltpu.VMEM((4, 32, 128), BF16),
             pltpu.VMEM((2, 128), F32),
             pltpu.VMEM((4, 2, 128), F32),
             pltpu.VMEM((2, 128), F32),
             pltpu.VMEM((4, 2, 128), F32),
-            pltpu.VMEM((8, 2, 128), F32),
+            pltpu.VMEM((4, 2, 128), F32),
             pltpu.VMEM((8, 512), BF16),
             pltpu.VMEM((4, 16, 128), BF16),
-            pltpu.SemaphoreType.REGULAR, pltpu.SemaphoreType.REGULAR,
+            pltpu.SemaphoreType.REGULAR((4,)), pltpu.SemaphoreType.REGULAR, pltpu.SemaphoreType.REGULAR,
             dma((2,)), dma((4,)), dma((4,)), dma, dma, dma,
-            dma, dma((3,)), dma, dma((2,)), dma((2,)), dma((2,)), dma((2,)), dma((2,)), dma((2,)), dma((2,)), dma, dma,
+            dma, dma((3,)), dma, dma((2,)), dma((2,)), dma((2,)), dma((2,)), dma((2,)), dma((2,)), dma, dma,
         ],
         compiler_params=pltpu.CompilerParams(collective_id=0, has_side_effects=True),
     )(

time: 29.3 us -> 28.1 us (0.959)
  the two profiles are of different devices: /device:TPU:16 before, /device:TPU:8 now
where the time goes in v4:
time: 28.1 us; the launch traced here: 28 us
  Pallas kernels  26.7 us (95%)
  between operations  1.29 us (5%)
    pallas_call x1, Pallas kernels, per_device(): pl.pallas_call(kernel, out_shape=[pltpu.VMEM(shape, BF16) for shape in sh...  25.9 us
    pallas_call x1, Pallas kernels, per_device(): pl.pallas_call(writer, out_shape=[pltpu.HBM(shape, BF16) for shape in sha...  0.73 us

profile of v4, /device:TPU:8, one launch (start us, length us, event | category | flops | bytes accessed | tf_op | source)
XLA Modules:
  0.0 28.0 jit_solution(4789221408541804779)
XLA Ops:
  1.3 25.9 %shard_map.129 = (bf16[1,320,128]{2,1,0:T(8,128)(2,1)S(1)}, bf16[1,320,128]{2,1,0:T(8,128)(2,1)S(1)}, bf16[1,320,128]{2,1,0:T(8,128)(2,1)S(1)}, bf16[1,4,320]{2,1,0:T(4,128)(2,1)S(1)}) custom-call(bf16[1,320,128]{2,1,0:T(8,128)(2,1)} %bitcast.9, bf16[1,320,128]{2,1,0:T(8,128)(2,1)} %bitcast.10, bf16[1,320,128]{2,1,0:T(8,128)(2,1)} %bitcast.11, ...), custom_call_target="tpu_custom_call" | custom-call | tf_op jit(solution)/shard_map/pallas_call | solution.py:332
  27.2 0.7 %shard_map.130 = (bf16[1,320,128]{2,1,0:T(8,128)(2,1)}, bf16[1,320,128]{2,1,0:T(8,128)(2,1)}, bf16[1,320,128]{2,1,0:T(8,128)(2,1)}, bf16[1,4,320]{2,1,0:T(4,128)(2,1)}) custom-call(bf16[1,320,128]{2,1,0:T(8,128)(2,1)S(1)} %get-tuple-element.12.refs_0_, bf16[1,320,128]{2,1,0:T(8,128)(2,1)S(1)} %get-tuple-element.13.refs_1_, ...), custom_call_target="tpu_custom_call" | custom-call | tf_op jit(solution)/shard_map/pallas_call | solution.py:367

commit v5 on v4

--- a/solution.py
+++ b/solution.py
@@ -62,8 +62,10 @@
     state, resident, tags, queries, keys, values, lengths,
     slabs, chosen, y_out, y_in, z_out, z_in, d_in, y_top, y_tops, z_top, z_tops, d_tops, attended, c_in,
     z_ready, s_ready, c_ready, small_sem, key_sem, value_sem, state_sem, resident_sem, tags_sem,
-    w_send, x_recv, s_recv, y_send, y_recv, z_send, z_recv, d_send, d_recv, c_send, c_recv,
+    x_recv, s_recv, y_recv, z_recv, d_recv, c_recv,
 ):
+    y_send, z_send, d_send = key_sem.at[0:2], key_sem.at[2:4], value_sem.at[0:2]
+    w_send, c_send = value_sem.at[2], value_sem.at[3]
     group = lax.axis_index("group")
     shard = lax.axis_index("shard")
     col = lax.axis_index("col")
@@ -125,35 +127,34 @@
         [jnp.concatenate([tall[0], blank], axis=1), jnp.concatenate([blank, tall[1]], axis=1)], axis=0
     )
     row_q = lax.broadcasted_iota(jnp.int32, (32, 2 * HS), 0) % 4
+    masked = [jnp.where(row_q == r, wide, 0.0).astype(BF16) for r in range(4)]
     row = lax.broadcasted_iota(jnp.int32, (32, 512), 0) % 4
+    position = shard * 512 + lax.broadcasted_iota(jnp.int32, (32, 512), 1)
+    l_load.wait()
+    limit = jnp.where(
+        row == 0, lengths[0, 0], jnp.where(row == 1, lengths[0, 1], jnp.where(row == 2, lengths[0, 2], lengths[0, 3]))
+    )
+    mask = position < limit
     scores = jnp.zeros((32, 512), F32)
     for r in range(4):
         k_loads[r].wait()
-        scores = scores + nt(jnp.where(row_q == r, wide, 0.0).astype(BF16), keys[r])
+        scores = scores + nt(masked[r], keys[r])
+    scores = jnp.where(mask, scores * (1.0 / HS**0.5), neg_big)
+    best = jnp.max(scores, axis=1, keepdims=True)
+    probs = jnp.exp(scores - best)
+    total = jnp.sum(probs, axis=1, keepdims=True)
+    weights = [jnp.where(row == r, probs, 0.0).astype(BF16) for r in range(4)]
+    y_top[...] = pack(best, total)
+    for copy in v_loads:
+        copy.wait()
     for i, src in enumerate((master_ref, grad_ref, first_ref, second_ref)):
         load(src.at[0], state.at[i], state_sem)
     r_load = load(resident_ref, resident, resident_sem)
     t_load = load(tags_ref, tags, tags_sem)
-
-    l_load.wait()
-    for copy in v_loads:
-        copy.wait()
-    position = shard * 512 + lax.broadcasted_iota(jnp.int32, (32, 512), 1)
-    limit = jnp.where(
-        row == 0, lengths[0, 0], jnp.where(row == 1, lengths[0, 1], jnp.where(row == 2, lengths[0, 2], lengths[0, 3]))
-    )
-    mask = position < limit
-    scores = scores * (1.0 / HS**0.5)
-    best = jnp.max(jnp.where(mask, scores, neg_big), axis=1, keepdims=True)
-    probs = jnp.where(mask, jnp.exp(scores - best), 0.0)
-    total = jnp.sum(probs, axis=1, keepdims=True)
-    both = jnp.zeros((32, 2 * HS), F32)
-    for r in range(4):
-        both = both + jnp.dot(
-            jnp.where(row == r, probs, 0.0).astype(BF16), values[r], preferred_element_type=F32
-        )
+    both = jnp.dot(
+        jnp.concatenate(weights, axis=1), values[...].reshape(2048, 2 * HS), preferred_element_type=F32
+    )
     y_out[...] = jnp.concatenate([both[:16, :HS], both[16:, HS:]], axis=0).astype(BF16)
-    y_top[...] = pack(best, total)
 
     told = jnp.where(late, 5, jnp.where(first, 0, 1))
     pl.semaphore_wait(barrier, 6 + core + told + before)
@@ -254,8 +255,8 @@
     odd = jnp.full((320, HS), tags[0], jnp.int32) % 2 == 1
     arrive(slabs.at[0:4], s_recv)
     for h in range(8):
-        place = (h % 2 * 4 + h // 2) * HS
-        chosen[:, place : place + HS] = jnp.where(odd, slabs[h], resident[0, :, h * HS : (h + 1) * HS])
+        place = h // 2 * HS
+        chosen[h % 2, place : place + HS, :] = jnp.where(odd, slabs[h], resident[0, :, h * HS : (h + 1) * HS]).T
 
     def finish(shares):
         acc, _ = merge(shares, last=True)
@@ -277,8 +278,8 @@
     pl.when(before < 3)(lambda: pl.semaphore_wait(c_ready, 3 - before))
     pl.when(first)(finish_first)
     pl.when(jnp.logical_not(first))(finish_other)
-    even = nt(attended[...], chosen[:, : 4 * HS])
-    uneven = nt(attended[...], chosen[:, 4 * HS :])
+    even = jnp.dot(attended[...], chosen[0], preferred_element_type=F32)
+    uneven = jnp.dot(attended[...], chosen[1], preferred_element_type=F32)
     share = even[:4] + uneven[4:]
     c_in[col] = jnp.concatenate(
         [
@@ -343,7 +344,7 @@
             pltpu.VMEM((4, 512, 256), BF16),
             pltpu.SMEM((1, 4), jnp.int32),
             pltpu.VMEM((8, 320, 128), BF16),
-            pltpu.VMEM((320, 1024), BF16),
+            pltpu.VMEM((2, 512, 320), BF16),
             pltpu.VMEM((32, 128), BF16),
             pltpu.VMEM((4, 32, 128), BF16),
             pltpu.VMEM((32, 128), BF16),
@@ -358,7 +359,7 @@
             pltpu.VMEM((4, 16, 128), BF16),
             pltpu.SemaphoreType.REGULAR((4,)), pltpu.SemaphoreType.REGULAR, pltpu.SemaphoreType.REGULAR,
             dma((2,)), dma((4,)), dma((4,)), dma, dma, dma,
-            dma, dma((3,)), dma, dma((2,)), dma((2,)), dma((2,)), dma((2,)), dma((2,)), dma((2,)), dma, dma,
+            dma((3,)), dma, dma((2,)), dma((2,)), dma((2,)), dma,
         ],
         compiler_params=pltpu.CompilerParams(collective_id=0, has_side_effects=True),
     )(

time: 28.1 us -> 28 us (level)
  no operation moved by 1% of the time
where the time goes in v5:
time: 28 us; the launch traced here: 27.8 us
  Pallas kernels  26.5 us (95%)
  between operations  1.29 us (5%)
    pallas_call x1, Pallas kernels, per_device(): pl.pallas_call(kernel, out_shape=[pltpu.VMEM(shape, BF16) for shape in sh...  25.8 us
    pallas_call x1, Pallas kernels, per_device(): pl.pallas_call(writer, out_shape=[pltpu.HBM(shape, BF16) for shape in sha...  0.73 us

profile of v5, /device:TPU:8, one launch (start us, length us, event | category | flops | bytes accessed | tf_op | source)
XLA Modules:
  0.0 27.8 jit_solution(18404916180337466545)
XLA Ops:
  1.3 25.8 %shard_map.129 = (bf16[1,320,128]{2,1,0:T(8,128)(2,1)S(1)}, bf16[1,320,128]{2,1,0:T(8,128)(2,1)S(1)}, bf16[1,320,128]{2,1,0:T(8,128)(2,1)S(1)}, bf16[1,4,320]{2,1,0:T(4,128)(2,1)S(1)}) custom-call(bf16[1,320,128]{2,1,0:T(8,128)(2,1)} %bitcast.9, bf16[1,320,128]{2,1,0:T(8,128)(2,1)} %bitcast.10, bf16[1,320,128]{2,1,0:T(8,128)(2,1)} %bitcast.11, ...), custom_call_target="tpu_custom_call" | custom-call | tf_op jit(solution)/shard_map/pallas_call | solution.py:333
  27.0 0.7 %shard_map.130 = (bf16[1,320,128]{2,1,0:T(8,128)(2,1)}, bf16[1,320,128]{2,1,0:T(8,128)(2,1)}, bf16[1,320,128]{2,1,0:T(8,128)(2,1)}, bf16[1,4,320]{2,1,0:T(4,128)(2,1)}) custom-call(bf16[1,320,128]{2,1,0:T(8,128)(2,1)S(1)} %get-tuple-element.12.refs_0_, bf16[1,320,128]{2,1,0:T(8,128)(2,1)S(1)} %get-tuple-element.13.refs_1_, ...), custom_call_target="tpu_custom_call" | custom-call | tf_op jit(solution)/shard_map/pallas_call | solution.py:368

commit v6 on v5

--- a/solution.py
+++ b/solution.py
@@ -61,7 +61,7 @@
     updated_ref, first_out, second_out, out_ref,
     state, resident, tags, queries, keys, values, lengths,
     slabs, chosen, y_out, y_in, z_out, z_in, d_in, y_top, y_tops, z_top, z_tops, d_tops, attended, c_in,
-    z_ready, s_ready, c_ready, small_sem, key_sem, value_sem, state_sem, resident_sem, tags_sem,
+    z_ready, s_ready, c_ready, x_ready, small_sem, key_sem, value_sem, state_sem, resident_sem, tags_sem,
     x_recv, s_recv, y_recv, z_recv, d_recv, c_recv,
 ):
     y_send, z_send, d_send = key_sem.at[0:2], key_sem.at[2:4], value_sem.at[0:2]
@@ -91,8 +91,10 @@
     def tell(sem, peer):
         pl.semaphore_signal(sem, inc=1, device_id=peer, device_id_type=MESH)
 
-    for peer in y_peers + x_peers:
+    for peer in y_peers:
         tell(barrier, peer)
+    for i in (1, 2, 3):
+        pl.when(x != i)(functools.partial(tell, barrier, {"group": 2 * i + core}))
     first, late = z == 0, z == 2
 
     def tell_first():
@@ -157,7 +159,7 @@
     y_out[...] = jnp.concatenate([both[:16, :HS], both[16:, HS:]], axis=0).astype(BF16)
 
     told = jnp.where(late, 5, jnp.where(first, 0, 1))
-    pl.semaphore_wait(barrier, 6 + core + told + before)
+    pl.semaphore_wait(barrier, 3 + jnp.where(x == 0, 0, 3) + core + told + before)
 
     def send_direct():
         def send_one(i, place):
@@ -175,6 +177,7 @@
         pl.when(z == j)(functools.partial(tell, z_ready.at[j], {"shard": y}))
     pl.when(late)(functools.partial(tell, z_ready.at[2], {"shard": 4 + y}))
     pl.when(core == 1)(functools.partial(tell, s_ready, sibling))
+    pl.when(x > 0)(functools.partial(tell, x_ready, {"group": core}))
     for d in (1, 2, 3):
         peer = {"col": jnp.where(z == 3, 3 - before + d, before - d)}
         pl.when(before >= d)(functools.partial(tell, c_ready, peer))
@@ -184,6 +187,7 @@
     arrive(state, state_sem)
     updated, first_new, second_new = adam(state[0], state[1], state[2], state[3])
     slabs[group] = updated
+    pl.when(x == 0)(lambda: pl.semaphore_wait(x_ready, 3))
     for d in (1, 3, 2):
         send(slabs.at[group], slabs.at[group], w_send, x_recv.at[d - 1], x_peers[d - 1])
     updated_ref[0] = updated
@@ -358,6 +362,7 @@
             pltpu.VMEM((8, 512), BF16),
             pltpu.VMEM((4, 16, 128), BF16),
             pltpu.SemaphoreType.REGULAR((4,)), pltpu.SemaphoreType.REGULAR, pltpu.SemaphoreType.REGULAR,
+            pltpu.SemaphoreType.REGULAR,
             dma((2,)), dma((4,)), dma((4,)), dma, dma, dma,
             dma((3,)), dma, dma((2,)), dma((2,)), dma((2,)), dma,
         ],

time: 28 us -> 27.7 us (0.989)
  the two profiles are of different devices: /device:TPU:8 before, /device:TPU:6 now
where the time goes in v6:
time: 27.7 us; the launch traced here: 27.3 us
  Pallas kernels  26 us (94%)
  between operations  1.29 us (5%)
    pallas_call x1, Pallas kernels, per_device(): pl.pallas_call(kernel, out_shape=[pltpu.VMEM(shape, BF16) for shape in sh...  25.3 us
    pallas_call x1, Pallas kernels, per_device(): pl.pallas_call(writer, out_shape=[pltpu.HBM(shape, BF16) for shape in sha...  0.73 us

profile of v6, /device:TPU:6, one launch (start us, length us, event | category | flops | bytes accessed | tf_op | source)
XLA Modules:
  0.0 27.3 jit_solution(1905015233836282201)
XLA Ops:
  1.3 25.3 %shard_map.129 = (bf16[1,320,128]{2,1,0:T(8,128)(2,1)S(1)}, bf16[1,320,128]{2,1,0:T(8,128)(2,1)S(1)}, bf16[1,320,128]{2,1,0:T(8,128)(2,1)S(1)}, bf16[1,4,320]{2,1,0:T(4,128)(2,1)S(1)}) custom-call(bf16[1,320,128]{2,1,0:T(8,128)(2,1)} %bitcast.9, bf16[1,320,128]{2,1,0:T(8,128)(2,1)} %bitcast.10, bf16[1,320,128]{2,1,0:T(8,128)(2,1)} %bitcast.11, ...), custom_call_target="tpu_custom_call" | custom-call | tf_op jit(solution)/shard_map/pallas_call | solution.py:337
  26.6 0.7 %shard_map.130 = (bf16[1,320,128]{2,1,0:T(8,128)(2,1)}, bf16[1,320,128]{2,1,0:T(8,128)(2,1)}, bf16[1,320,128]{2,1,0:T(8,128)(2,1)}, bf16[1,4,320]{2,1,0:T(4,128)(2,1)}) custom-call(bf16[1,320,128]{2,1,0:T(8,128)(2,1)S(1)} %get-tuple-element.12.refs_0_, bf16[1,320,128]{2,1,0:T(8,128)(2,1)S(1)} %get-tuple-element.13.refs_1_, ...), custom_call_target="tpu_custom_call" | custom-call | tf_op jit(solution)/shard_map/pallas_call | solution.py:373

commit v7 on v6

--- a/solution.py
+++ b/solution.py
@@ -64,8 +64,8 @@
     z_ready, s_ready, c_ready, x_ready, small_sem, key_sem, value_sem, state_sem, resident_sem, tags_sem,
     x_recv, s_recv, y_recv, z_recv, d_recv, c_recv,
 ):
-    y_send, z_send, d_send = key_sem.at[0:2], key_sem.at[2:4], value_sem.at[0:2]
-    w_send, c_send = value_sem.at[2], value_sem.at[3]
+    y_send, z_send, d_send = key_sem.at[0:2], key_sem.at[2:4], small_sem
+    w_send, c_send = state_sem, value_sem
     group = lax.axis_index("group")
     shard = lax.axis_index("shard")
     col = lax.axis_index("col")
@@ -111,7 +111,7 @@
         peer = {"col": jnp.where(z == 3, 3 - before - d, before + d)}
         pl.when(before + d < 4)(functools.partial(tell, barrier, peer))
 
-    v_loads = [load(values_ref.at[0, r], values.at[r], value_sem.at[r]) for r in range(4)]
+    v_load = load(values_ref.at[0], values, value_sem)
 
     def send(src, dst, send_sem, recv_sem, peer):
         pltpu.make_async_remote_copy(
@@ -147,8 +147,7 @@
     total = jnp.sum(probs, axis=1, keepdims=True)
     weights = [jnp.where(row == r, probs, 0.0).astype(BF16) for r in range(4)]
     y_top[...] = pack(best, total)
-    for copy in v_loads:
-        copy.wait()
+    v_load.wait()
     for i, src in enumerate((master_ref, grad_ref, first_ref, second_ref)):
         load(src.at[0], state.at[i], state_sem)
     r_load = load(resident_ref, resident, resident_sem)
@@ -363,7 +362,7 @@
             pltpu.VMEM((4, 16, 128), BF16),
             pltpu.SemaphoreType.REGULAR((4,)), pltpu.SemaphoreType.REGULAR, pltpu.SemaphoreType.REGULAR,
             pltpu.SemaphoreType.REGULAR,
-            dma((2,)), dma((4,)), dma((4,)), dma, dma, dma,
+            dma((2,)), dma((4,)), dma, dma, dma, dma,
             dma((3,)), dma, dma((2,)), dma((2,)), dma((2,)), dma,
         ],
         compiler_params=pltpu.CompilerParams(collective_id=0, has_side_effects=True),

time: 27.7 us -> 27.7 us (level)
  no operation moved by 1% of the time
where the time goes in v7:
time: 27.7 us; the launch traced here: 27.3 us
  Pallas kernels  26 us (94%)
  between operations  1.29 us (5%)
    pallas_call x1, Pallas kernels, per_device(): pl.pallas_call(kernel, out_shape=[pltpu.VMEM(shape, BF16) for shape in sh...  25.3 us
    pallas_call x1, Pallas kernels, per_device(): pl.pallas_call(writer, out_shape=[pltpu.HBM(shape, BF16) for shape in sha...  0.73 us

profile of v7, /device:TPU:6, one launch (start us, length us, event | category | flops | bytes accessed | tf_op | source)
XLA Modules:
  0.0 27.3 jit_solution(1183095572696076913)
XLA Ops:
  1.3 25.3 %shard_map.129 = (bf16[1,320,128]{2,1,0:T(8,128)(2,1)S(1)}, bf16[1,320,128]{2,1,0:T(8,128)(2,1)S(1)}, bf16[1,320,128]{2,1,0:T(8,128)(2,1)S(1)}, bf16[1,4,320]{2,1,0:T(4,128)(2,1)S(1)}) custom-call(bf16[1,320,128]{2,1,0:T(8,128)(2,1)} %bitcast.9, bf16[1,320,128]{2,1,0:T(8,128)(2,1)} %bitcast.10, bf16[1,320,128]{2,1,0:T(8,128)(2,1)} %bitcast.11, ...), custom_call_target="tpu_custom_call" | custom-call | tf_op jit(solution)/shard_map/pallas_call | solution.py:336
  26.6 0.7 %shard_map.130 = (bf16[1,320,128]{2,1,0:T(8,128)(2,1)}, bf16[1,320,128]{2,1,0:T(8,128)(2,1)}, bf16[1,320,128]{2,1,0:T(8,128)(2,1)}, bf16[1,4,320]{2,1,0:T(4,128)(2,1)}) custom-call(bf16[1,320,128]{2,1,0:T(8,128)(2,1)S(1)} %get-tuple-element.12.refs_0_, bf16[1,320,128]{2,1,0:T(8,128)(2,1)S(1)} %get-tuple-element.13.refs_1_, ...), custom_call_target="tpu_custom_call" | custom-call | tf_op jit(solution)/shard_map/pallas_call | solution.py:372

commit v8 on v6

--- a/solution.py
+++ b/solution.py
@@ -85,7 +85,7 @@
 
     q_load = load(queries_ref, queries, small_sem.at[0])
     l_load = load(lengths_ref, lengths, small_sem.at[1])
-    k_loads = [load(keys_ref.at[0, r], keys.at[r], key_sem.at[r]) for r in range(4)]
+    k_loads = [load(keys_ref.at[0, r], keys.at[:, 256 * r : 256 * r + 256], key_sem.at[r]) for r in range(4)]
     barrier = pltpu.get_barrier_semaphore()
 
     def tell(sem, peer):
@@ -137,10 +137,9 @@
         row == 0, lengths[0, 0], jnp.where(row == 1, lengths[0, 1], jnp.where(row == 2, lengths[0, 2], lengths[0, 3]))
     )
     mask = position < limit
-    scores = jnp.zeros((32, 512), F32)
-    for r in range(4):
-        k_loads[r].wait()
-        scores = scores + nt(masked[r], keys[r])
+    for copy in k_loads:
+        copy.wait()
+    scores = nt(jnp.concatenate(masked, axis=1), keys[...])
     scores = jnp.where(mask, scores * (1.0 / HS**0.5), neg_big)
     best = jnp.max(scores, axis=1, keepdims=True)
     probs = jnp.exp(scores - best)
@@ -344,7 +343,7 @@
             pltpu.VMEM((1, 320, 1024), BF16),
             pltpu.SMEM((1,), jnp.int32),
             pltpu.VMEM((1, 4, 1024), BF16),
-            pltpu.VMEM((4, 512, 256), BF16),
+            pltpu.VMEM((512, 1024), BF16),
             pltpu.VMEM((4, 512, 256), BF16),
             pltpu.SMEM((1, 4), jnp.int32),
             pltpu.VMEM((8, 320, 128), BF16),

time: 27.7 us -> 27.7 us (level)
  no operation moved by 1% of the time
where the time goes in v8:
time: 27.7 us; the launch traced here: 27.5 us
  Pallas kernels  26.2 us (95%)
  between operations  1.29 us (5%)
    pallas_call x1, Pallas kernels, per_device(): pl.pallas_call(kernel, out_shape=[pltpu.VMEM(shape, BF16) for shape in sh...  25.5 us
    pallas_call x1, Pallas kernels, per_device(): pl.pallas_call(writer, out_shape=[pltpu.HBM(shape, BF16) for shape in sha...  0.73 us

profile of v8, /device:TPU:6, one launch (start us, length us, event | category | flops | bytes accessed | tf_op | source)
XLA Modules:
  0.0 27.5 jit_solution(1187768288744421879)
XLA Ops:
  1.3 25.5 %shard_map.129 = (bf16[1,320,128]{2,1,0:T(8,128)(2,1)S(1)}, bf16[1,320,128]{2,1,0:T(8,128)(2,1)S(1)}, bf16[1,320,128]{2,1,0:T(8,128)(2,1)S(1)}, bf16[1,4,320]{2,1,0:T(4,128)(2,1)S(1)}) custom-call(bf16[1,320,128]{2,1,0:T(8,128)(2,1)} %bitcast.9, bf16[1,320,128]{2,1,0:T(8,128)(2,1)} %bitcast.10, bf16[1,320,128]{2,1,0:T(8,128)(2,1)} %bitcast.11, ...), custom_call_target="tpu_custom_call" | custom-call | tf_op jit(solution)/shard_map/pallas_call | solution.py:336
  26.8 0.7 %shard_map.130 = (bf16[1,320,128]{2,1,0:T(8,128)(2,1)}, bf16[1,320,128]{2,1,0:T(8,128)(2,1)}, bf16[1,320,128]{2,1,0:T(8,128)(2,1)}, bf16[1,4,320]{2,1,0:T(4,128)(2,1)}) custom-call(bf16[1,320,128]{2,1,0:T(8,128)(2,1)S(1)} %get-tuple-element.12.refs_0_, bf16[1,320,128]{2,1,0:T(8,128)(2,1)S(1)} %get-tuple-element.13.refs_1_, ...), custom_call_target="tpu_custom_call" | custom-call | tf_op jit(solution)/shard_map/pallas_call | solution.py:372
